TPU v7x, 128 devices: a whole 4x4x4 slice. The times are simulated.
128 devices in a mesh: dp: 32 (over x_hi, z, y), tensor: 4 (over x_lo, core).
Axes of the slice: x: 4 (x_hi: 2, x_lo: 2; x = x_hi * 2 + x_lo), y: 4, z: 4, core: 2. Of those that a mesh axis runs over, the one named last changes fastest.
Arguments:
- routes: int32 [16384, 8], P(('dp', 'tensor')), may hold values from 0 to 127, all different within a row; in each aligned block of 128 rows (0 to 127, 128 to 255, ...) at most 12 rows name the same one
- gate_values: bfloat16 [16384, 8], P(('dp', 'tensor')), may hold values from 0.049804688 to 0.5
- grad_out: bfloat16 [16384, 4096], P(('dp', 'tensor')), may hold values from -0.29882812 to 0.29882812
- hidden: bfloat16 [128, 1536, 768], P(('dp', 'tensor')), may hold values from -6 to 6
- w_down: bfloat16 [128, 768, 4096], P(('dp', 'tensor')), may hold values from -0.21875 to 0.21875
Outputs:
- grad_gates: float32 [16384, 8], P(('dp', 'tensor'))
- grad_hidden: bfloat16 [128, 1536, 768], P(('dp', 'tensor'))
- grad_down: bfloat16 [128, 768, 4096], P(('dp', 'tensor'))
Inputs may be any that keep to these rules, and one draw needn't show every extreme that they name: `routes`: the 8 ids of a token differ. Among the tokens of one device no expert is named more than 12 times, and in every draw some expert is named exactly 12 times by the tokens of some device.
All inputs are finite; a program needn't handle non-finite values.
Results may differ from a plain program's by a relative error of at most 0.0049.
Values may be sent and summed in bfloat16 or wider, within the bound.
A program may use at most 128 MiB of HBM per device.

v0:
```python
import jax
import jax.numpy as jnp
from jax import lax
from jax.sharding import PartitionSpec as P


def local(routes, gate_values, grad_out, hidden, w_down):
    experts = lax.axis_size(("dp", "tensor"))
    tok_count = routes.shape[0]
    top_count = routes.shape[1]
    capacity = hidden.shape[1] // experts
    model_width = grad_out.shape[1]
    flat_routes = routes.reshape(-1)
    onehot = (flat_routes[:, None] == jnp.arange(experts, dtype=jnp.int32)[None, :]).astype(
        jnp.int32
    )
    earlier = jnp.cumsum(onehot, axis=0) - onehot
    slot_index = jnp.sum(earlier * onehot, axis=1)
    target = flat_routes * capacity + slot_index
    pair_count = tok_count * top_count
    pair_ids = jnp.arange(pair_count, dtype=jnp.int32)
    token_table = (
        jnp.full((experts * capacity,), tok_count, jnp.int32).at[target].set(pair_ids // top_count)
    )
    pair_table = jnp.full((experts * capacity,), pair_count, jnp.int32).at[target].set(pair_ids)
    padded_rows = jnp.concatenate([grad_out, jnp.zeros((1, model_width), grad_out.dtype)], axis=0)
    padded_gates = jnp.concatenate([gate_values.reshape(-1), jnp.zeros((1,), gate_values.dtype)])
    send_rows = jnp.take(padded_rows, token_table, axis=0).reshape(experts, capacity, model_width)
    send_gates = jnp.take(padded_gates, pair_table).reshape(experts, capacity)
    weight_slab = w_down[0]
    stored = hidden[0]
    direct_rows, direct_gates = (
        lax.all_to_all(send_rows, ("dp", "tensor"), split_axis=0, concat_axis=0, tiled=True),
        lax.all_to_all(send_gates, ("dp", "tensor"), split_axis=0, concat_axis=0, tiled=True),
    )
    recv_gates = direct_gates.reshape(experts * capacity)
    recv_rows = direct_rows.reshape(experts * capacity, model_width)
    back_proj = lax.dot_general(
        recv_rows, weight_slab, (((1,), (1,)), ((), ())), preferred_element_type=jnp.float32
    )
    scaled_rows = (recv_gates.astype(jnp.float32)[:, None] * recv_rows.astype(jnp.float32)).astype(
        jnp.bfloat16
    )
    back_proj, scaled_rows = (back_proj, scaled_rows)
    slot_grad = jnp.sum(stored.astype(jnp.float32) * back_proj, axis=1)
    hidden_grad = (recv_gates.astype(jnp.float32)[:, None] * back_proj).astype(jnp.bfloat16)
    weight_grad = lax.dot_general(
        stored, scaled_rows, (((0,), (0,)), ((), ())), preferred_element_type=jnp.float32
    ).astype(jnp.bfloat16)
    returned = lax.all_to_all(
        slot_grad.reshape(experts, capacity),
        ("dp", "tensor"),
        split_axis=0,
        concat_axis=0,
        tiled=True,
    )
    grad_gates = returned.reshape(-1)[target].reshape(tok_count, top_count)
    return (grad_gates, hidden_grad[None], weight_grad[None])


def solution(mesh):
    in_specs = (
        P(("dp", "tensor"), None),
        P(("dp", "tensor"), None),
        P(("dp", "tensor"), None),
        P(("dp", "tensor"), None, None),
        P(("dp", "tensor"), None, None),
    )
    out_specs = (
        P(("dp", "tensor"), None),
        P(("dp", "tensor"), None, None),
        P(("dp", "tensor"), None, None),
    )
    return jax.shard_map(local, mesh=mesh, in_specs=in_specs, out_specs=out_specs, check_vma=False)
```

profile of v0, /device:TPU:1, one launch (start us, length us, event | category | flops | bytes accessed | tf_op | source)
XLA Modules:
  0.0 435.5 jit_solution(4105270196952514258)
XLA Ops:
  0.6 0.8 copy.23
  3.4 4.3 scatter_custom_fusion.1
  7.7 0.8 copy.28
  8.7 9.5 %gather_fusion.2 = bf16[1536]{0:T(1024)(128)(2,1)S(1)} fusion(bf16[1025]{0:T(1024)(128)(2,1)S(1)} %pad_maximum_fusion, s32[2048]{0:T(1024)S(1)} %pad_clamp_fusion), kind=kCustom, calls=%fused_computation.2 | custom fusion | bytes 12288 | tf_op jit(solution)/shard_map/jit(_take)/gather | solution.py:29
  18.1 0.8 select_n.53
  18.9 11.5 %all-to-all-start.2 = ((bf16[128,1,12]{2,1,0:T(2,128)(2,1)}), bf16[128,1,12]{2,1,0:T(2,128)(2,1)S(1)}, u32[]{:S(2)}, u32[]{:S(2)}) async-start(bf16[128,1,12]{2,1,0:T(2,128)(2,1)} %select_n.53), calls=%async_computation.2 | async-start | bytes 131072 | tf_op jit(solution)/shard_map/all_to_all | solution.py:34
  30.4 4.3 scatter_custom_fusion
  34.8 1.3 concatenate.6
  36.1 9.5 %gather_fusion = bf16[1536,4096]{1,0:T(8,128)(2,1)} fusion(bf16[129,4096]{1,0:T(8,128)(2,1)S(1)} %concatenate.6, s32[2048]{0:T(1024)S(1)} %pad_clamp_fusion.1), kind=kCustom, calls=%fused_computation | custom fusion | bytes 25171968 | tf_op jit(solution)/shard_map/jit(_take)/gather | solution.py:28
  45.7 17.9 %gather.14 = bf16[128,12,4096]{2,1,0:T(8,128)(2,1)} reshape(bf16[1536,4096]{1,0:T(8,128)(2,1)} %gather_fusion) | data formatting | bytes 25165824 | tf_op jit(solution)/shard_map/jit(_take)/gather | solution.py:28
  63.7 14.1 %broadcast_select_fusion = bf16[128,12,4096]{2,1,0:T(8,128)(2,1)} fusion(bf16[128,12,4096]{2,1,0:T(8,128)(2,1)} %gather.14, pred[128,12]{1,0:T(8,128)(4,1)S(1)} %broadcast_in_dim.42), kind=kLoop, calls=%fused_computation.6 | loop fusion | flops 6291456 | bytes 25167360 | tf_op jit(solution)/shard_map/jit(_take)/select_n | solution.py:28
  77.8 10.2 %all-to-all-start = ((bf16[128,12,4096]{2,1,0:T(8,128)(2,1)}), bf16[128,12,4096]{2,1,0:T(8,128)(2,1)}, u32[]{:S(2)}, u32[]{:S(2)}) async-start(bf16[128,12,4096]{2,1,0:T(8,128)(2,1)} %broadcast_select_fusion), calls=%async_computation | async-start | bytes 33554432 | tf_op jit(solution)/shard_map/all_to_all | solution.py:33
  88.0 2.4 copy.21
  90.9 215.5 %all-to-all-done = bf16[128,12,4096]{2,1,0:T(8,128)(2,1)} async-done(((bf16[128,12,4096]{2,1,0:T(8,128)(2,1)}), bf16[128,12,4096]{2,1,0:T(8,128)(2,1)}, u32[]{:S(2)}, u32[]{:S(2)}) %all-to-all-start) | async-done | bytes 12582944 | tf_op jit(solution)/shard_map/all_to_all | solution.py:33
  306.4 18.2 %reshape.129 = bf16[1536,4096]{1,0:T(8,128)(2,1)} reshape(bf16[128,12,4096]{2,1,0:T(8,128)(2,1)} %all-to-all-done) | data formatting | bytes 25165824 | tf_op jit(solution)/shard_map/reshape | solution.py:37
  324.6 16.2 %fusion.3 = (bf16[1,1536,768]{1,2,0:T(8,128)(2,1)}, f32[1536]{0:T(1024)S(1)}) fusion(f32[1536]{0:T(1024)S(1)} %reshape.133, bf16[1,1536,768]{1,2,0:T(8,128)(2,1)} %copy.21, bf16[1536,4096]{1,0:T(8,128)(2,1)} %reshape.129, bf16[1,768,4096]{2,1,0:T(8,128)(2,1)} %param.9), kind=kOutput, calls=%fused_computation.13 | convolution fusion | flops 9669572608 | bytes 23605248 | tf_op jit(solution)/shard_map/dot_general | solution.py:38
  341.5 24.4 %all-to-all-start.1 = ((f32[128,1,12]{2,1,0:T(1,128)}), f32[128,1,12]{2,1,0:T(1,128)S(1)}, u32[]{:S(2)}, u32[]{:S(2)}) async-start(f32[128,1,12]{2,1,0:T(1,128)} %bitcast.7), calls=%async_computation.1 | async-start | bytes 131072 | tf_op jit(solution)/shard_map/all_to_all | solution.py:50
  365.9 15.3 %multiply_convert_fusion = bf16[128,12,4096]{2,1,0:T(8,128)(2,1)} fusion(bf16[128,12,4096]{2,1,0:T(8,128)(2,1)} %all-to-all-done, f32[128,12]{1,0:T(8,128)S(1)} %bitcast.32), kind=kLoop, calls=%fused_computation.5 | loop fusion | flops 18874368 | bytes 25171968 | tf_op jit(solution)/shard_map/convert_element_type | solution.py:41
  381.2 18.2 %convert_element_type.56 = bf16[1536,4096]{1,0:T(8,128)(2,1)} reshape(bf16[128,12,4096]{2,1,0:T(8,128)(2,1)} %multiply_convert_fusion) | data formatting | bytes 25165824 | tf_op jit(solution)/shard_map/convert_element_type | solution.py:41
  399.4 14.9 %fusion.2 = bf16[1,768,4096]{1,2,0:T(8,128)(2,1)} fusion(bf16[1536,4096]{1,0:T(8,128)(2,1)} %convert_element_type.56, bf16[1,1536,768]{2,1,0:T(8,128)(2,1)S(1)} %copy-done), kind=kOutput, calls=%fused_computation.10 | convolution fusion | flops 9666822144 | bytes 21233664 | tf_op jit(solution)/shard_map/dot_general | solution.py:47
  414.2 4.3 copy.31
  418.5 8.6 %copy.32 = bf16[1,768,4096]{2,1,0:T(8,128)(2,1)} copy(bf16[1,768,4096]{1,2,0:T(8,128)(2,1)} %fusion.2) | data formatting | bytes 12582912
  427.6 0.8 reduce.7
  428.5 6.2 %gather_fusion.1 = f32[1024]{0:T(1024)S(1)} fusion(f32[1536]{0:T(1024)S(1)} %reshape.130, s32[1024]{0:T(1024)S(1)} %broadcast_clamp_fusion), kind=kCustom, calls=%fused_computation.1 | custom fusion | bytes 12288 | tf_op jit(solution)/shard_map/gather | solution.py:57
  (38 shorter events, 4.6 us)
Async XLA Ops:
  18.9 58.9 %all-to-all-start.2 = ((bf16[128,1,12]{2,1,0:T(2,128)(2,1)}), bf16[128,1,12]{2,1,0:T(2,128)(2,1)S(1)}, u32[]{:S(2)}, u32[]{:S(2)}) async-start(bf16[128,1,12]{2,1,0:T(2,128)(2,1)} %select_n.53), calls=%async_computation.2 | async-start | bytes 131072 | tf_op jit(solution)/shard_map/all_to_all | solution.py:34
  77.8 10.2 %copy-start = (bf16[1,1536,768]{2,1,0:T(8,128)(2,1)S(1)}, bf16[1,1536,768]{2,1,0:T(8,128)(2,1)}, u32[]{:S(2)}) copy-start(bf16[1,1536,768]{2,1,0:T(8,128)(2,1)} %param.8) | copy-start | bytes 7077892
  77.8 228.6 %all-to-all-start = ((bf16[128,12,4096]{2,1,0:T(8,128)(2,1)}), bf16[128,12,4096]{2,1,0:T(8,128)(2,1)}, u32[]{:S(2)}, u32[]{:S(2)}) async-start(bf16[128,12,4096]{2,1,0:T(8,128)(2,1)} %broadcast_select_fusion), calls=%async_computation | async-start | bytes 33554432 | tf_op jit(solution)/shard_map/all_to_all | solution.py:33
  341.5 85.6 %all-to-all-start.1 = ((f32[128,1,12]{2,1,0:T(1,128)}), f32[128,1,12]{2,1,0:T(1,128)S(1)}, u32[]{:S(2)}, u32[]{:S(2)}) async-start(f32[128,1,12]{2,1,0:T(1,128)} %bitcast.7), calls=%async_computation.1 | async-start | bytes 131072 | tf_op jit(solution)/shard_map/all_to_all | solution.py:50
where the time goes:
time: 438 us; the launch traced here: 435 us
  waiting for transfers between devices  216 us (49%)
  local copies, waits for them, and re-layouts  110 us (25%)
  starting transfers between devices  46.1 us (11%)
  other arithmetic  31.9 us (7%)
  matrix products  31 us (7%)
    all_to_all x1, waiting for transfers between devices, local(): lax.all_to_all(send_rows, ('dp', 'tensor'), split_axis=0, concat_axis=0,...  216 us
    gather x2, local copies, waits for them, and re-layouts, local(): jnp.take(padded_rows, token_table, axis=0)  27.4 us
    all_to_all x1, starting transfers between devices, local(): lax.all_to_all(slot_grad.reshape(experts, capacity), ('dp', 'tensor'), sp...  24.4 us
    convert_element_type x1, local copies, waits for them, and re-layouts, local(): (recv_gates.astype(jnp.float32)[:, None] * recv_rows.astype(jnp.float32))...  18.2 us
    reshape x1, local copies, waits for them, and re-layouts, local(): recv_rows = direct_rows.reshape(experts * capacity, model_width)  18.2 us
    unnamed x8, local copies, waits for them, and re-layouts  17.6 us
    dot_general x1, matrix products, local(): lax.dot_general(recv_rows, weight_slab, (((1,), (1,)), ((), ())), preferr...  16.2 us
    convert_element_type x1, other arithmetic, local(): (recv_gates.astype(jnp.float32)[:, None] * recv_rows.astype(jnp.float32))...  15.3 us
  transfers between devices with their start and end apart: 3, of which 1 were waited for; matrix products, arithmetic and copies ran while one was open for 26% of the time, Pallas kernels for 0%

commit v1 on v0

v1 whole, which is shorter than its diff:
```python
import itertools

import jax
import jax.numpy as jnp
import numpy as np
from jax import lax
from jax.experimental import pallas as pl
from jax.experimental.pallas import tpu as pltpu
from jax.sharding import PartitionSpec as P

MESH = pl.DeviceIdType.MESH
F32 = jnp.float32
BF16 = jnp.bfloat16

DEV = 128
TOK = 128
CAP = 12
TOP = 8
LANE = 128
SEATS = 8
BLOCKS = 16
ROWS = SEATS * CAP


def half(v):
    return lax.div(v, 2)


def odd(v):
    return lax.rem(v, 2)


def near(k, v):
    return (1 - k) * (v + 1 - 2 * odd(v)) + k * (3 - v)


def far(k, v):
    return (1 - k) * (3 - v) + k * (v + 1 - 2 * odd(v))


def seat(k, v):
    return (1 - k) * odd(v) + k * half(v)


def pair(k, v):
    return (1 - k) * half(v) + k * odd(v + half(v))


def place(chip, core):
    x, y, z = chip
    return half(x) * 16 + z * 4 + y, odd(x) * 2 + core


def number(chip, core):
    dp, tensor = place(chip, core)
    return dp * 4 + tensor


def reach(k, chip, n):
    return tuple(far(k, v) if (n >> d) & 1 else v for d, v in enumerate(chip))


def block_of(k, chip, n):
    total = k * 8
    for d, v in enumerate(chip):
        own = pair(k, v)
        total = total + (1 << d) * ((1 - own) if (n >> d) & 1 else own)
    return total


def row_orders():
    natural = np.zeros(DEV * CAP, np.int32)
    for k, b, m in itertools.product(range(2), range(8), range(8)):
        chip = []
        for d in range(3):
            p, s = (b >> d) & 1, (m >> d) & 1
            chip.append((2 * p + s) if k == 0 else (2 * s + (p ^ s)))
        x, y, z = chip
        device = ((x // 2) * 16 + z * 4 + y) * 4 + (x % 2) * 2 + k
        first = ((k * 8 + b) * 8 + m) * CAP
        natural[first : first + CAP] = device * CAP + np.arange(CAP)
    kernel_row = np.argsort(natural).astype(np.int32)
    return natural, kernel_row


def iota(shape, dim):
    return lax.broadcasted_iota(jnp.int32, shape, dim)


def dot(a, b, dims=((1,), (0,))):
    return lax.dot_general(a, b, (dims, ((), ())), preferred_element_type=F32)


def ones_where(mask):
    return jnp.where(mask, 1.0, 0.0).astype(BF16)


def expand(first, gates_all, counts_all):
    row = iota((ROWS, LANE), 0)
    of = (row * 171) >> 11
    slot = (row - of * CAP).astype(F32)
    pick = ones_where(iota((ROWS, LANE), 1) == of + first)
    gates = dot(pick, gates_all)
    counts = dot(pick, counts_all)
    hit = (counts == slot) & (gates > 0.0)
    return hit, gates, of


def kernel(
    chunks,
    routes_ref,
    routes_t_ref,
    gates_t_ref,
    natural_ref,
    kernel_row_ref,
    grad_ref,
    hidden_ref,
    weight_ref,
    grad_gates_ref,
    grad_hidden_ref,
    grad_down_ref,
    tok,
    stage,
    recv,
    weight,
    hid,
    hid_k,
    hid_t,
    back,
    gcol,
    select,
    gate_f,
    gate_out,
    gate_in,
    scaled,
    down,
    sg_out,
    sg_in,
    sg_pack,
    sg_all,
    in_sem,
    rep_send,
    rep_recv,
    row_send,
    row_recv,
    gate_send,
    gate_recv,
    sg_send,
    sg_recv,
    ret_send,
    ret_recv,
    down_sem,
    hid_sem,
):
    width = recv.shape[3]
    model = weight.shape[1]
    ffe = weight.shape[0]
    dp = lax.axis_index("dp")
    tensor = lax.axis_index("tensor")
    k = odd(tensor)
    chip = (half(tensor) + 2 * lax.div(dp, 16), lax.rem(dp, 4), lax.rem(lax.div(dp, 4), 4))
    seats = tuple(seat(k, v) for v in chip)
    mine = seats[0] + 2 * seats[1] + 4 * seats[2]
    my_block = block_of(k, chip, 0)
    cores = (k, 1 - k)
    order = [(n, rc) for n in (1, 2, 4, 3, 5, 6, 7, 0) for rc in (0, 1) if (n, rc) != (0, 0)]

    def receiver(n, rc):
        return reach(k, chip, n), cores[rc]

    def sender(n, rc):
        return reach(cores[rc], chip, n), cores[rc]

    def member(flips):
        return tuple(near(k, v) if (flips >> d) & 1 else v for d, v in enumerate(chip))

    load_rows = pltpu.make_async_copy(grad_ref, tok.at[mine, :, pl.ds(0, model)], in_sem.at[0])
    load_rows.start()
    load_hidden = pltpu.make_async_copy(hidden_ref, hid, in_sem.at[1])
    load_hidden.start()
    load_weight = pltpu.make_async_copy(weight_ref, weight, in_sem.at[2])
    load_weight.start()

    barrier = pltpu.get_barrier_semaphore()
    greet = [(member(f), k) for f in range(1, 8)]
    greet += [receiver(n, rc) for n, rc in order]
    greet += [sender(n, 1) for n in range(1, 8)]
    for who, core in greet:
        pl.semaphore_signal(barrier, inc=1, device_id=place(who, core), device_id_type=MESH)

    table = jnp.zeros((DEV, TOK), F32)
    for c in range(TOP):
        named = iota((DEV, TOK), 0) == routes_t_ref[c : c + 1, :]
        table = table + jnp.where(named, gates_t_ref[c : c + 1, :], 0.0)
    tok[mine, :, pl.ds(model, LANE)] = table.astype(BF16)
    load_rows.wait()
    pl.semaphore_wait(barrier, len(greet))

    part = (model + LANE) // 3
    steps = {}
    for p in range(3):
        for s in range(3):
            axis = (p + s) % 3
            done = [(p + i) % 3 for i in range(s)]
            copies = []
            for c in range(1 << s):
                slot = 0
                for d in range(3):
                    flip = d in done and (c >> done.index(d)) & 1
                    slot = slot + (1 << d) * ((1 - seats[d]) if flip else seats[d])
                ref = tok.at[slot, :, pl.ds(p * part, part)]
                at = p * 7 + (1 << s) - 1 + c
                copies.append(
                    pltpu.make_async_remote_copy(
                        src_ref=ref,
                        dst_ref=ref,
                        send_sem=rep_send.at[at],
                        recv_sem=rep_recv.at[at],
                        device_id=place(member(1 << axis), k),
                        device_id_type=MESH,
                    )
                )
            steps[p, s] = copies
    for s in range(3):
        for p in range(3):
            if s:
                for copy in steps[p, s - 1]:
                    copy.wait_recv()
            for copy in steps[p, s]:
                copy.start()

    load_hidden.wait()
    span = 2 * LANE

    @pl.loop(0, DEV * CAP // span)
    def _(i):
        first = pl.multiple_of(i * span, span)
        move = ones_where(kernel_row_ref[0:1, :] == iota((span, DEV * CAP), 0) + first)
        moved = dot(move, hid[...])
        hid_k[pl.ds(first, span), :] = moved.astype(BF16)
        hid_t[:, pl.ds(first, span)] = moved.T.astype(BF16)

    for p in range(3):
        for copy in steps[p, 2]:
            copy.wait_recv()

    gate_f[...] = tok[:, :, pl.ds(model, LANE)].astype(F32)
    for n in range(8):
        for rc in range(2):
            expert = number(*receiver(n, rc))
            for m in range(SEATS):
                gate_out[n * 2 + rc, m : m + 1, :] = gate_f[m, pl.ds(expert, 1), :]
    gate_in[my_block] = gate_out[0]

    def gate_copy(n, rc):
        d = n * 2 + rc
        return pltpu.make_async_remote_copy(
            src_ref=gate_out.at[d],
            dst_ref=gate_in.at[my_block],
            send_sem=gate_send.at[d],
            recv_sem=gate_recv.at[my_block],
            device_id=place(*receiver(n, rc)),
            device_id_type=MESH,
        )

    for n, rc in order:
        gate_copy(n, rc).start()

    earlier = ones_where(iota((TOK, TOK), 0) < iota((TOK, TOK), 1))
    gates_all = gate_out[...].reshape(BLOCKS * SEATS, TOK)
    counts_all = dot(ones_where(gates_all > 0.0), earlier).astype(BF16)
    gates_all = gates_all.astype(BF16)
    quad = ROWS // 2

    for d in range(BLOCKS):
        hit, _, of = expand(d * SEATS, gates_all, counts_all)
        for h in range(2):
            rows = slice(h * quad, (h + 1) * quad)
            for m in range(4):
                chosen = hit[rows] & (of[rows] == 4 * h + m)
                select[h, d, :, m * TOK : (m + 1) * TOK] = ones_where(chosen)

    def row_copy(q, n, rc):
        d = n * 2 + rc
        return pltpu.make_async_remote_copy(
            src_ref=stage.at[q, d],
            dst_ref=recv.at[q, my_block],
            send_sem=row_send.at[q, d],
            recv_sem=row_recv.at[q, my_block],
            device_id=place(*receiver(n, rc)),
            device_id_type=MESH,
        )

    @pl.loop(0, chunks)
    def _(q):
        first = pl.multiple_of(q * width, width)
        for h in range(2):
            source = tok[4 * h : 4 * h + 4, :, pl.ds(first, width)].reshape(4 * TOK, width)
            picked = dot(select[h].reshape(BLOCKS * quad, 4 * TOK), source).astype(BF16)
            picked = picked.reshape(BLOCKS, quad, width)
            stage[q, :, h * quad : (h + 1) * quad, :] = picked
            recv[q, my_block, h * quad : (h + 1) * quad, :] = picked[0]
        for n, rc in order:
            row_copy(q, n, rc).start()

    for n, rc in order:
        b = block_of(cores[rc], chip, n)
        pltpu.make_async_copy(gate_in.at[b], gate_in.at[b], gate_recv.at[b]).wait()
    gates_all = gate_in[...].reshape(BLOCKS * SEATS, TOK)
    counts_all = dot(ones_where(gates_all > 0.0), earlier).astype(BF16)
    gates_all = gates_all.astype(BF16)
    for b in range(BLOCKS):
        hit, gates, _ = expand(b * SEATS, gates_all, counts_all)
        column = jnp.sum(jnp.where(hit, gates, 0.0), axis=1, keepdims=True)
        gcol[b] = jnp.broadcast_to(column, (ROWS, LANE))

    back[...] = jnp.zeros_like(back)
    load_weight.wait()

    def down_copy(q, slot):
        first = pl.multiple_of(q * width, width)
        return pltpu.make_async_copy(
            down.at[slot], grad_down_ref.at[:, pl.ds(first, width)], down_sem.at[slot]
        )

    some = BLOCKS // 2

    @pl.loop(0, chunks)
    def _(q):
        first = pl.multiple_of(q * width, width)
        slot = odd(q)
        for n, rc in order:
            b = block_of(cores[rc], chip, n)
            pltpu.make_async_copy(recv.at[q, b], recv.at[q, b], row_recv.at[q, b]).wait()

        @pl.loop(0, 2)
        def _(i):
            got = recv[q, pl.ds(i * some, some)].reshape(some * ROWS, width)
            back[pl.ds(i * some, some)] += dot(
                got, weight[:, pl.ds(first, width)], ((1,), (1,))
            ).reshape(some, ROWS, ffe)

        @pl.loop(0, BLOCKS)
        def _(b):
            wide = jnp.concatenate([gcol[b]] * (width // LANE), axis=1)
            scaled[pl.ds(b * ROWS, ROWS), :] = (recv[q, b].astype(F32) * wide).astype(BF16)

        @pl.when(q >= 2)
        def _():
            down_copy(q - 2, slot).wait()

        @pl.loop(0, width // span)
        def _(i):
            at = pl.multiple_of(i * span, span)
            down[slot, :, pl.ds(at, span)] = dot(hid_t[...], scaled[:, pl.ds(at, span)]).astype(
                BF16
            )

        down_copy(q, slot).start()

    @pl.loop(0, BLOCKS)
    def _(b):
        rows = pl.ds(b * ROWS, ROWS)
        total = back[b]
        slots = jnp.sum(hid_k[rows, :].astype(F32) * total, axis=1, keepdims=True)
        wide = jnp.concatenate([gcol[b]] * (ffe // LANE), axis=1)
        hid_k[rows, :] = (total * wide).astype(BF16)
        row = iota((ROWS, LANE), 0)
        lane = row + 4 * ((row * 171) >> 11)
        line = jnp.sum(jnp.where(iota((ROWS, LANE), 1) == lane, slots, 0.0), axis=0, keepdims=True)
        sg_out[b] = jnp.broadcast_to(line, (8, LANE))

    def slot_copy(n, rc):
        d = n * 2 + rc
        b = block_of(cores[rc], chip, n)
        return pltpu.make_async_remote_copy(
            src_ref=sg_out.at[b],
            dst_ref=sg_in.at[d],
            send_sem=sg_send.at[d],
            recv_sem=sg_recv.at[d],
            device_id=place(*sender(n, rc)),
            device_id_type=MESH,
        )

    for n, rc in order:
        slot_copy(n, rc).start()
    sg_in[0] = sg_out[my_block]

    @pl.loop(0, DEV * CAP // span)
    def _(i):
        first = pl.multiple_of(i * span, span)
        move = ones_where(natural_ref[0:1, :] == iota((span, DEV * CAP), 0) + first)
        hid[pl.ds(first, span), :] = dot(move, hid_k[...]).astype(BF16)

    store_hidden = pltpu.make_async_copy(hid, grad_hidden_ref, hid_sem.at[0])
    store_hidden.start()

    for n, rc in order:
        slot_copy(n, rc).wait_recv()
    for d in range(BLOCKS):
        sg_pack[d : d + 1, :] = sg_in[d, 0:1, :]

    def return_copy(f):
        return pltpu.make_async_remote_copy(
            src_ref=sg_pack,
            dst_ref=sg_all.at[mine],
            send_sem=ret_send.at[f],
            recv_sem=ret_recv.at[f],
            device_id=place(member(f), k),
            device_id_type=MESH,
        )

    for f in range(1, 8):
        return_copy(f).start()
    sg_all[mine] = sg_pack[...]

    column = iota((1, LANE), 1)
    chips = []
    for d in range(3):
        s = (column >> (4 + d)) & 1
        p = pair(k, chip[d])
        v = (1 - k) * (2 * p + s) + k * (2 * s + ((s + p) & 1))
        n = (column >> (1 + d)) & 1
        across = (1 - k) * (3 - v) + k * (v + 1 - 2 * (v & 1))
        chips.append(n * across + (1 - n) * v)
    x, y, z = chips
    other = column & 1
    core = other * (1 - k) + (1 - other) * k
    expert = ((x >> 1) * 16 + z * 4 + y) * 4 + (x & 1) * 2 + core
    named = [expert == routes_ref[:, c : c + 1] for c in range(TOP)]
    any_named = named[0]
    for mask in named[1:]:
        any_named = any_named | mask
    before = ones_where(iota((TOK, TOK), 1) < iota((TOK, TOK), 0))
    count = dot(before, ones_where(any_named))

    for f in range(1, 8):
        return_copy(f).wait_recv()
    turned = sg_all[...].reshape(SEATS * BLOCKS, LANE).T
    gate_f[0] = turned
    slots = gate_f[0, pl.ds(pl.multiple_of(mine * 16, 16), 16), :]
    value = jnp.zeros((TOK, LANE), F32)
    for j in range(CAP):
        value = value + jnp.where(count == float(j), slots[j : j + 1, :], 0.0)
    grad_gates_ref[...] = jnp.concatenate(
        [jnp.sum(jnp.where(mask, value, 0.0), axis=1, keepdims=True) for mask in named], axis=1
    )

    for copies in steps.values():
        for copy in copies:
            copy.wait_send()
    for n, rc in order:
        gate_copy(n, rc).wait_send()
        slot_copy(n, rc).wait_send()

    @pl.loop(0, chunks)
    def _(q):
        for n, rc in order:
            row_copy(q, n, rc).wait_send()

    for f in range(1, 8):
        return_copy(f).wait_send()
    for q in (chunks - 2, chunks - 1):
        down_copy(q, q % 2).wait()
    store_hidden.wait()


def local(routes, gate_values, grad_out, hidden, w_down):
    model = grad_out.shape[1]
    ffe = hidden.shape[2]
    slots = DEV * CAP
    width = 512
    chunks = model // width
    natural, kernel_row = (jnp.asarray(np.tile(v[None], (8, 1))) for v in row_orders())
    vmem = pl.BlockSpec(memory_space=pltpu.VMEM)
    hbm = pl.BlockSpec(memory_space=pl.ANY)
    dma = pltpu.SemaphoreType.DMA

    def body(*refs):
        kernel(chunks, *refs)

    grad_gates, grad_hidden, grad_down = pl.pallas_call(
        body,
        out_shape=(
            jax.ShapeDtypeStruct((TOK, TOP), F32),
            jax.ShapeDtypeStruct((slots, ffe), BF16),
            jax.ShapeDtypeStruct((ffe, model), BF16),
        ),
        in_specs=[vmem] * 5 + [hbm] * 3,
        out_specs=(vmem, hbm, hbm),
        scratch_shapes=[
            pltpu.VMEM((SEATS, TOK, model + LANE), BF16),
            pltpu.VMEM((chunks, BLOCKS, ROWS, width), BF16),
            pltpu.VMEM((chunks, BLOCKS, ROWS, width), BF16),
            pltpu.VMEM((ffe, model), BF16),
            pltpu.VMEM((slots, ffe), BF16),
            pltpu.VMEM((slots, ffe), BF16),
            pltpu.VMEM((ffe, slots), BF16),
            pltpu.VMEM((BLOCKS, ROWS, ffe), F32),
            pltpu.VMEM((BLOCKS, ROWS, LANE), F32),
            pltpu.VMEM((2, BLOCKS, ROWS // 2, 4 * TOK), BF16),
            pltpu.VMEM((SEATS, DEV, TOK), F32),
            pltpu.VMEM((BLOCKS, SEATS, TOK), F32),
            pltpu.VMEM((BLOCKS, SEATS, TOK), F32),
            pltpu.VMEM((slots, width), BF16),
            pltpu.VMEM((2, ffe, width), BF16),
            pltpu.VMEM((BLOCKS, 8, LANE), F32),
            pltpu.VMEM((BLOCKS, 8, LANE), F32),
            pltpu.VMEM((BLOCKS, LANE), F32),
            pltpu.VMEM((SEATS, BLOCKS, LANE), F32),
            dma((3,)),
            dma((21,)),
            dma((21,)),
            dma((chunks, BLOCKS)),
            dma((chunks, BLOCKS)),
            dma((BLOCKS,)),
            dma((BLOCKS,)),
            dma((BLOCKS,)),
            dma((BLOCKS,)),
            dma((8,)),
            dma((8,)),
            dma((2,)),
            dma((1,)),
        ],
        compiler_params=pltpu.CompilerParams(
            collective_id=0, has_side_effects=True, vmem_limit_bytes=63 * 1024 * 1024
        ),
        cost_estimate=pl.CostEstimate(
            flops=4 * slots * ffe * model, bytes_accessed=20_000_000, transcendentals=0
        ),
    )(
        routes,
        routes.T,
        gate_values.T.astype(F32),
        natural,
        kernel_row,
        grad_out,
        hidden[0],
        w_down[0],
    )
    return grad_gates, grad_hidden[None], grad_down[None]


def solution(mesh):
    both = ("dp", "tensor")
    in_specs = (P(both, None), P(both, None), P(both, None), P(both, None, None), P(both, None, None))
    out_specs = (P(both, None), P(both, None, None), P(both, None, None))
    return jax.shard_map(local, mesh=mesh, in_specs=in_specs, out_specs=out_specs, check_vma=False)
```

time: 438 us -> 156 us (0.36)
  waiting for transfers between devices: 216 us -> 0 us
  Pallas kernels: 0 us -> 140 us
  local copies, waits for them, and re-layouts: 110 us -> 12.4 us
  starting transfers between devices: 46.1 us -> 0 us
  matrix products: 31 us -> 0 us
  other arithmetic: 31.9 us -> 1.28 us
    all_to_all x3 -> x0, waiting for transfers between devices: 216 us -> none  [the longest x1 216 us: local(): lax.all_to_all(send_rows, ('dp', 'tensor'), split_axis=0, concat_axis=0,...]
    pallas_call x0 -> x1, Pallas kernels: none -> 140 us  [local(): pl.pallas_call(body, out_shape=(jax.ShapeDtypeStruct((TOK, TOP), F32), ja...]
    all_to_all x3 -> x0, starting transfers between devices: 46.1 us -> none  [the longest x1 24.4 us: local(): lax.all_to_all(slot_grad.reshape(experts, capacity), ('dp', 'tensor'), sp...]
    gather x4 -> x0, local copies, waits for them, and re-layouts: 43 us -> none  [the longest x2 27.4 us: local(): jnp.take(padded_rows, token_table, axis=0)]
    dot_general x2 -> x0, matrix products: 31 us -> none  [the longest x1 16.2 us: local(): lax.dot_general(recv_rows, weight_slab, (((1,), (1,)), ((), ())), preferr...]
    reshape x4 -> x0, local copies, waits for them, and re-layouts: 18.5 us -> none  [the longest x1 18.2 us: local(): recv_rows = direct_rows.reshape(experts * capacity, model_width)]
    convert_element_type x2 -> x0, local copies, waits for them, and re-layouts: 18.3 us -> none  [the longest x1 18.2 us: local(): (recv_gates.astype(jnp.float32)[:, None] * recv_rows.astype(jnp.float32))...]
    convert_element_type x3 -> x1, other arithmetic: 15.5 us -> 1.28 us  [local(): gate_values.T.astype(F32)]
  transfers between devices with their start and end apart: 3 -> 0, of which waited for: 1 -> 0; matrix products, arithmetic and copies ran while one was open for 26% -> 0% of each run, Pallas kernels for 0% -> 0%
where the time goes in v1:
time: 156 us; the launch traced here: 155 us
  Pallas kernels  140 us (90%)
  local copies, waits for them, and re-layouts  12.4 us (8%)
    pallas_call x1, Pallas kernels, local(): pl.pallas_call(body, out_shape=(jax.ShapeDtypeStruct((TOK, TOP), F32), ja...  140 us
    unnamed x4, local copies, waits for them, and re-layouts  12.4 us

profile of v1, /device:TPU:1, one launch (start us, length us, event | category | flops | bytes accessed | tf_op | source)
XLA Modules:
  0.0 154.7 jit_solution(8386087289333367253)
XLA Ops:
  0.6 1.3 convert_bitcast_fusion.refs_2_
  1.9 1.4 copy.10.refs_0_
  3.3 140.4 %shard_map.94 = (f32[128,8]{1,0:T(8,128)}, bf16[1536,768]{1,0:T(8,128)(2,1)}, bf16[768,4096]{1,0:T(8,128)(2,1)}) custom-call(s32[128,8]{1,0:T(8,128)} %copy.10.refs_0_, s32[8,128]{1,0:T(8,128)} %bitcast.9, f32[8,128]{1,0:T(8,128)} %convert_bitcast_fusion.refs_2_, s32[8,1536]{1,0:T(8,128)} %constant.4.clone.refs_3_, s32[8,1536]{1,0:T(8,128)} %constant.5.clone.refs_4_, ...), custom_call_target="tpu_custom_call" | custom-call | flops 19327352832 | bytes 20000000 | tf_op jit(solution)/shard_map/pallas_call | solution.py:482
  143.7 1.5 copy.11
  145.2 3.2 %copy.14 = bf16[1,1536,768]{2,1,0:T(8,128)(2,1)} copy(bf16[1,1536,768]{2,1,0:T(8,128)(2,1)} %bitcast.8) | data formatting | bytes 4718592
  148.4 6.3 %copy.15 = bf16[1,768,4096]{2,1,0:T(8,128)(2,1)} copy(bf16[1,768,4096]{2,1,0:T(8,128)(2,1)} %bitcast.7) | data formatting | bytes 12582912

commit v2 on v1

v2 whole, which is shorter than its diff:
```python
import itertools

import jax
import jax.numpy as jnp
import numpy as np
from jax import lax
from jax.experimental import pallas as pl
from jax.experimental.pallas import tpu as pltpu
from jax.sharding import PartitionSpec as P

MESH = pl.DeviceIdType.MESH
F32 = jnp.float32
BF16 = jnp.bfloat16

DEV = 128
TOK = 128
CAP = 12
TOP = 8
LANE = 128
SEATS = 8
BLOCKS = 16
ROWS = SEATS * CAP


def half(v):
    return lax.div(v, 2)


def odd(v):
    return lax.rem(v, 2)


def near(k, v):
    return (1 - k) * (v + 1 - 2 * odd(v)) + k * (3 - v)


def far(k, v):
    return (1 - k) * (3 - v) + k * (v + 1 - 2 * odd(v))


def seat(k, v):
    return (1 - k) * odd(v) + k * half(v)


def pair(k, v):
    return (1 - k) * half(v) + k * odd(v + half(v))


def place(chip, core):
    x, y, z = chip
    return half(x) * 16 + z * 4 + y, odd(x) * 2 + core


def number(chip, core):
    dp, tensor = place(chip, core)
    return dp * 4 + tensor


def reach(k, chip, n):
    return tuple(far(k, v) if (n >> d) & 1 else v for d, v in enumerate(chip))


def block_of(k, chip, n):
    total = k * 8
    for d, v in enumerate(chip):
        own = pair(k, v)
        total = total + (1 << d) * ((1 - own) if (n >> d) & 1 else own)
    return total


def row_orders():
    natural = np.zeros(DEV * CAP, np.int32)
    for k, b, m in itertools.product(range(2), range(8), range(8)):
        chip = []
        for d in range(3):
            p, s = (b >> d) & 1, (m >> d) & 1
            chip.append((2 * p + s) if k == 0 else (2 * s + (p ^ s)))
        x, y, z = chip
        device = ((x // 2) * 16 + z * 4 + y) * 4 + (x % 2) * 2 + k
        first = ((k * 8 + b) * 8 + m) * CAP
        natural[first : first + CAP] = device * CAP + np.arange(CAP)
    return natural


def iota(shape, dim):
    return lax.broadcasted_iota(jnp.int32, shape, dim)


def dot(a, b, dims=((1,), (0,))):
    return lax.dot_general(a, b, (dims, ((), ())), preferred_element_type=F32)


def ones_where(mask):
    return jnp.where(mask, 1.0, 0.0).astype(BF16)


def expand(first, gates_all, counts_all):
    row = iota((ROWS, LANE), 0)
    of = (row * 171) >> 11
    slot = (row - of * CAP).astype(F32)
    pick = ones_where(iota((ROWS, LANE), 1) == of + first)
    gates = dot(pick, gates_all)
    counts = dot(pick, counts_all)
    hit = (counts == slot) & (gates > 0.0)
    return hit, gates, of


def kernel(
    chunks,
    routes_ref,
    gates_ref,
    kernel_row_ref,
    grad_ref,
    hidden_ref,
    weight_ref,
    grad_gates_ref,
    grad_hidden_ref,
    grad_down_ref,
    tok,
    stage,
    recv,
    weight,
    hid,
    hid_k,
    hid_t,
    back,
    natural,
    gcol,
    select,
    tables,
    gate_f,
    gate_out,
    gate_in,
    scaled,
    down,
    sg_out,
    sg_in,
    sg_pack,
    sg_all,
    owner,
    count,
    in_sem,
    tab_send,
    tab_recv,
    rep_send,
    rep_recv,
    row_send,
    row_recv,
    gate_send,
    gate_recv,
    sg_send,
    sg_recv,
    ret_send,
    ret_recv,
    down_sem,
    hid_sem,
):
    width = recv.shape[3]
    model = weight.shape[1]
    ffe = weight.shape[0]
    dp = lax.axis_index("dp")
    tensor = lax.axis_index("tensor")
    k = odd(tensor)
    chip = (half(tensor) + 2 * lax.div(dp, 16), lax.rem(dp, 4), lax.rem(lax.div(dp, 4), 4))
    seats = tuple(seat(k, v) for v in chip)
    mine = seats[0] + 2 * seats[1] + 4 * seats[2]
    my_block = block_of(k, chip, 0)
    cores = (k, 1 - k)
    order = [(n, rc) for n in (1, 2, 4, 3, 5, 6, 7, 0) for rc in (0, 1) if (n, rc) != (0, 0)]

    def receiver(n, rc):
        return reach(k, chip, n), cores[rc]

    def sender(n, rc):
        return reach(cores[rc], chip, n), cores[rc]

    def member(flips):
        return tuple(near(k, v) if (flips >> d) & 1 else v for d, v in enumerate(chip))

    to_id = {key: place(*receiver(*key)) for key in order}
    from_id = {key: place(*sender(*key)) for key in order}
    from_block = {(n, rc): block_of(cores[rc], chip, n) for n, rc in order}
    member_id = {f: place(member(f), k) for f in range(1, 8)}

    load_rows = pltpu.make_async_copy(grad_ref, tok.at[mine], in_sem.at[0])
    load_rows.start()
    load_hidden = pltpu.make_async_copy(hidden_ref, hid, in_sem.at[1])
    load_hidden.start()
    load_weight = pltpu.make_async_copy(weight_ref, weight, in_sem.at[2])
    load_weight.start()

    barrier = pltpu.get_barrier_semaphore()
    greet = list(member_id.values()) + list(to_id.values())
    greet += [from_id[n, 1] for n in range(1, 8)]
    for who in greet:
        pl.semaphore_signal(barrier, inc=1, device_id=who, device_id_type=MESH)

    gates_t = gates_ref[...].astype(F32)
    table = jnp.zeros((DEV, TOK), F32)
    for c in range(TOP):
        named = iota((DEV, TOK), 0) == routes_ref[c : c + 1, :]
        table = table + jnp.where(named, gates_t[c : c + 1, :], 0.0)
    tables[mine] = table.astype(BF16)
    load_rows.wait()
    pl.semaphore_wait(barrier, len(greet))

    def table_copy(f):
        return pltpu.make_async_remote_copy(
            src_ref=tables.at[mine],
            dst_ref=tables.at[mine],
            send_sem=tab_send.at[f],
            recv_sem=tab_recv.at[f],
            device_id=member_id[f],
            device_id_type=MESH,
        )

    tiles = model // LANE
    parts = [(0, 11), (11, 11), (22, tiles - 22)]

    def rep_copy(p, h, c):
        slot = 0
        for d in range(3):
            hop = (d - p) % 3
            slot = slot + (1 << d) * ((1 - seats[d]) if hop < h and (c >> hop) & 1 else seats[d])
        at = p * 7 + (1 << h) - 1 + c
        ref = tok.at[slot, :, pl.ds(parts[p][0] * LANE, parts[p][1] * LANE)]
        return pltpu.make_async_remote_copy(
            src_ref=ref,
            dst_ref=ref,
            send_sem=rep_send.at[at],
            recv_sem=rep_recv.at[at],
            device_id=member_id[1 << ((p + h) % 3)],
            device_id_type=MESH,
        )

    def own(p):
        for h in range(3):
            rep_copy(p, h, 0).start()

    def forward_first(p):
        rep_copy(p, 0, 0).wait_recv()
        rep_copy(p, 1, 1).start()
        rep_copy(p, 2, 1).start()
        rep_copy(p, 1, 0).wait_recv()
        rep_copy(p, 2, 2).start()

    def forward_last(p):
        rep_copy(p, 1, 1).wait_recv()
        rep_copy(p, 2, 3).start()

    def complete(p):
        for c in range(4):
            rep_copy(p, 2, c).wait_recv()

    for f in range(1, 8):
        table_copy(f).start()
    for p in range(3):
        own(p)

    for f in range(1, 8):
        table_copy(f).wait_recv()
    gate_f[...] = tables[...].astype(F32)
    for n in range(8):
        for rc in range(2):
            expert = number(*receiver(n, rc))
            for m in range(SEATS):
                gate_out[n * 2 + rc, m : m + 1, :] = gate_f[m, pl.ds(expert, 1), :]
    gate_in[my_block] = gate_out[0]

    def gate_copy(n, rc):
        d = n * 2 + rc
        return pltpu.make_async_remote_copy(
            src_ref=gate_out.at[d],
            dst_ref=gate_in.at[my_block],
            send_sem=gate_send.at[d],
            recv_sem=gate_recv.at[my_block],
            device_id=to_id[n, rc],
            device_id_type=MESH,
        )

    for n, rc in order:
        gate_copy(n, rc).start()

    for p in range(3):
        forward_first(p)

    earlier = ones_where(iota((TOK, TOK), 0) < iota((TOK, TOK), 1))
    gates_all = gate_out[...].reshape(BLOCKS * SEATS, TOK)
    counts_all = dot(ones_where(gates_all > 0.0), earlier).astype(BF16)
    gates_all = gates_all.astype(BF16)
    quad = ROWS // 2

    @pl.loop(0, BLOCKS)
    def _(d):
        hit, _, of = expand(d * SEATS, gates_all, counts_all)
        for h in range(2):
            rows = slice(h * quad, (h + 1) * quad)
            for m in range(4):
                chosen = hit[rows] & (of[rows] == 4 * h + m)
                select[h, d, :, m * TOK : (m + 1) * TOK] = ones_where(chosen)

    load_hidden.wait()
    span = 2 * LANE

    def permute_hidden(start, stop):
        @pl.loop(start, stop)
        def _(i):
            first = pl.multiple_of(i * span, span)
            move = ones_where(kernel_row_ref[0:1, :] == iota((span, DEV * CAP), 0) + first)
            moved = dot(move, hid[...])
            hid_k[pl.ds(first, span), :] = moved.astype(BF16)
            hid_t[:, pl.ds(first, span)] = moved.T.astype(BF16)

    permute_hidden(0, 2)
    for p in range(3):
        forward_last(p)
    permute_hidden(2, 6)

    def row_copy(q, n, rc):
        d = n * 2 + rc
        return pltpu.make_async_remote_copy(
            src_ref=stage.at[q, d],
            dst_ref=recv.at[q, my_block],
            send_sem=row_send.at[q],
            recv_sem=row_recv.at[q],
            device_id=to_id[n, rc],
            device_id_type=MESH,
        )

    def exchange(start, stop):
        @pl.loop(start, stop)
        def _(q):
            first = pl.multiple_of(q * width, width)
            for h in range(2):
                source = tok[4 * h : 4 * h + 4, :, pl.ds(first, width)].reshape(4 * TOK, width)
                picked = dot(select[h].reshape(BLOCKS * quad, 4 * TOK), source).astype(BF16)
                picked = picked.reshape(BLOCKS, quad, width)
                stage[q, :, h * quad : (h + 1) * quad, :] = picked
                recv[q, my_block, h * quad : (h + 1) * quad, :] = picked[0]
            for n, rc in order:
                row_copy(q, n, rc).start()

    complete(0)
    ready = [p[0] * LANE // width for p in parts] + [chunks]
    exchange(ready[0], ready[1])

    for n, rc in order:
        b = from_block[n, rc]
        pltpu.make_async_copy(gate_in.at[b], gate_in.at[b], gate_recv.at[b]).wait()
    gates_all = gate_in[...].reshape(BLOCKS * SEATS, TOK)
    counts_all = dot(ones_where(gates_all > 0.0), earlier).astype(BF16)
    gates_all = gates_all.astype(BF16)
    @pl.loop(0, BLOCKS)
    def _(b):
        hit, gates, _ = expand(b * SEATS, gates_all, counts_all)
        column = jnp.sum(jnp.where(hit, gates, 0.0), axis=1, keepdims=True)
        gcol[b] = jnp.broadcast_to(column, (ROWS, LANE))

    complete(1)
    exchange(ready[1], ready[2])
    complete(2)
    exchange(ready[2], ready[3])

    line = iota((LANE, TOK), 0)
    chips = []
    for d in range(3):
        s = (line >> (4 + d)) & 1
        p = pair(k, chip[d])
        v = (1 - k) * (2 * p + s) + k * (2 * s + ((s + p) & 1))
        n = (line >> (1 + d)) & 1
        across = (1 - k) * (3 - v) + k * (v + 1 - 2 * (v & 1))
        chips.append(n * across + (1 - n) * v)
    x, y, z = chips
    other = line & 1
    core = other * (1 - k) + (1 - other) * k
    expert = ((x >> 1) * 16 + z * 4 + y) * 4 + (x & 1) * 2 + core
    owner[...] = expert
    any_named = expert == routes_ref[0:1, :]
    for c in range(1, TOP):
        any_named = any_named | (expert == routes_ref[c : c + 1, :])
    count[...] = dot(ones_where(any_named), earlier)

    back[...] = jnp.zeros_like(back)
    load_weight.wait()

    def down_copy(q, slot):
        first = pl.multiple_of(q * width, width)
        return pltpu.make_async_copy(
            down.at[slot], grad_down_ref.at[:, pl.ds(first, width)], down_sem.at[slot]
        )

    some = BLOCKS // 2

    def project(q):
        first = pl.multiple_of(q * width, width)
        all_rows = recv.at[q, pl.ds(0, BLOCKS - 1)]
        pltpu.make_async_copy(all_rows, all_rows, row_recv.at[q]).wait()

        @pl.loop(0, 2)
        def _(i):
            got = recv[q, pl.ds(i * some, some)].reshape(some * ROWS, width)
            back[pl.ds(i * some, some)] += dot(
                got, weight[:, pl.ds(first, width)], ((1,), (1,))
            ).reshape(some, ROWS, ffe)

    def weight_grad(q, slot):
        @pl.loop(0, BLOCKS)
        def _(b):
            wide = jnp.concatenate([gcol[b]] * (width // LANE), axis=1)
            scaled[pl.ds(b * ROWS, ROWS), :] = (recv[q, b].astype(F32) * wide).astype(BF16)

        down[slot] = dot(hid_t[...], scaled[...]).astype(BF16)
        down_copy(q, slot).start()

    @pl.loop(0, chunks - 1)
    def _(q):
        slot = odd(q)
        project(q)

        @pl.when(q >= 2)
        def _():
            down_copy(q - 2, slot).wait()

        weight_grad(q, slot)

    project(chunks - 1)

    @pl.loop(0, BLOCKS)
    def _(b):
        slots = hid_k[pl.ds(b * ROWS, ROWS), :].astype(F32) * back[b]
        slots = jnp.sum(slots, axis=1, keepdims=True)
        row = iota((ROWS, LANE), 0)
        lane = row + 4 * ((row * 171) >> 11)
        line = jnp.sum(jnp.where(iota((ROWS, LANE), 1) == lane, slots, 0.0), axis=0, keepdims=True)
        sg_out[b] = jnp.broadcast_to(line, (8, LANE))

    def slot_copy(n, rc):
        d = n * 2 + rc
        b = from_block[n, rc]
        return pltpu.make_async_remote_copy(
            src_ref=sg_out.at[b],
            dst_ref=sg_in.at[d],
            send_sem=sg_send.at[d],
            recv_sem=sg_recv.at[d],
            device_id=from_id[n, rc],
            device_id_type=MESH,
        )

    for n, rc in order:
        slot_copy(n, rc).start()
    sg_in[0] = sg_out[my_block]

    last = (chunks - 1) % 2
    down_copy(chunks - 3, last).wait()
    weight_grad(chunks - 1, last)

    for n, rc in order:
        slot_copy(n, rc).wait_recv()
    for d in range(BLOCKS):
        sg_pack[d : d + 1, :] = sg_in[d, 0:1, :]

    def return_copy(f):
        return pltpu.make_async_remote_copy(
            src_ref=sg_pack,
            dst_ref=sg_all.at[mine],
            send_sem=ret_send.at[f],
            recv_sem=ret_recv.at[f],
            device_id=member_id[f],
            device_id_type=MESH,
        )

    for f in range(1, 8):
        return_copy(f).start()
    sg_all[mine] = sg_pack[...]

    for kk in range(2):

        @pl.loop(0, 4)
        def _(i):
            for px in range(2):
                b = kk * 8 + px + 2 * i
                wide = jnp.concatenate([gcol[b]] * (ffe // LANE), axis=1)
                total = back[b] * wide
                for m in range(SEATS):
                    x, y, z = (
                        (s + 2 * p) if kk == 0 else (p + s * (3 - 2 * p))
                        for p, s in zip((px, odd(i), half(i)), (m & 1, (m >> 1) & 1, m >> 2))
                    )
                    first = CAP * ((x % 2) * 2 + kk)
                    natural[(x // 2) * 16 + z * 4 + y, first : first + CAP, :] = total[
                        m * CAP : (m + 1) * CAP
                    ]

    hid[...] = natural[...].reshape(DEV * CAP, ffe).astype(BF16)
    store_hidden = pltpu.make_async_copy(hid, grad_hidden_ref, hid_sem.at[0])
    store_hidden.start()

    for p in range(3):
        for h in range(3):
            for c in range(1 << h):
                rep_copy(p, h, c).wait_send()
    for n, rc in order:
        gate_copy(n, rc).wait_send()
        slot_copy(n, rc).wait_send()

    @pl.loop(0, chunks)
    def _(q):
        all_rows = stage.at[q, pl.ds(1, BLOCKS - 1)]
        pltpu.make_async_copy(all_rows, all_rows, row_send.at[q]).wait()

    for f in range(1, 8):
        table_copy(f).wait_send()
        return_copy(f).wait_send()

    for f in range(1, 8):
        return_copy(f).wait_recv()
    values = pltpu.roll(sg_all[...].reshape(LANE, LANE), LANE - 16 * mine, 1)
    value = jnp.zeros((LANE, TOK), F32)
    for j in range(CAP):
        value = value + jnp.where(count[...] == float(j), values[:, j : j + 1], 0.0)
    for c in range(TOP):
        named = owner[...] == routes_ref[c : c + 1, :]
        grad_gates_ref[c : c + 1, :] = jnp.sum(jnp.where(named, value, 0.0), axis=0, keepdims=True)

    down_copy(chunks - 2, 1 - last).wait()
    down_copy(chunks - 1, last).wait()
    store_hidden.wait()


def finish(hidden_ref, down_ref, grad_hidden_ref, grad_down_ref, hidden, down, sems):
    pieces = 6
    loads, stores = [], []
    for source, held, target in (
        (down_ref, down, grad_down_ref),
        (hidden_ref, hidden, grad_hidden_ref),
    ):
        rows = source.shape[0] // pieces
        for i in range(pieces):
            at = pl.ds(i * rows, rows)
            n = len(loads)
            loads.append(pltpu.make_async_copy(source.at[at], held.at[at], sems.at[0, n]))
            stores.append(pltpu.make_async_copy(held.at[at], target.at[at], sems.at[1, n]))
            loads[-1].start()
    for load, store in zip(loads, stores):
        load.wait()
        store.start()
    for store in stores:
        store.wait()


def local(routes, gate_values, grad_out, hidden, w_down):
    model = grad_out.shape[1]
    ffe = hidden.shape[2]
    slots = DEV * CAP
    width = 256
    chunks = model // width
    kernel_row = jnp.asarray(np.tile(np.argsort(row_orders())[None], (8, 1)), jnp.int32)
    vmem = pl.BlockSpec(memory_space=pltpu.VMEM)
    hbm = pl.BlockSpec(memory_space=pl.ANY)
    dma = pltpu.SemaphoreType.DMA

    def body(*refs):
        kernel(chunks, *refs)

    grad_gates, grad_hidden, grad_down = pl.pallas_call(
        body,
        out_shape=(
            jax.ShapeDtypeStruct((TOP, TOK), F32),
            jax.ShapeDtypeStruct((slots, ffe), BF16),
            jax.ShapeDtypeStruct((ffe, model), BF16),
        ),
        in_specs=[vmem] * 3 + [hbm] * 3,
        out_specs=(vmem, hbm, hbm),
        scratch_shapes=[
            pltpu.VMEM((SEATS, TOK, model), BF16),
            pltpu.VMEM((chunks, BLOCKS, ROWS, width), BF16),
            pltpu.VMEM((chunks, BLOCKS, ROWS, width), BF16),
            pltpu.VMEM((ffe, model), BF16),
            pltpu.VMEM((slots, ffe), BF16),
            pltpu.VMEM((slots, ffe), BF16),
            pltpu.VMEM((ffe, slots), BF16),
            pltpu.VMEM((BLOCKS, ROWS, ffe), F32),
            pltpu.VMEM((DEV // 4, 4 * CAP, ffe), F32),
            pltpu.VMEM((BLOCKS, ROWS, LANE), F32),
            pltpu.VMEM((2, BLOCKS, ROWS // 2, 4 * TOK), BF16),
            pltpu.VMEM((SEATS, DEV, TOK), BF16),
            pltpu.VMEM((SEATS, DEV, TOK), F32),
            pltpu.VMEM((BLOCKS, SEATS, TOK), F32),
            pltpu.VMEM((BLOCKS, SEATS, TOK), F32),
            pltpu.VMEM((slots, width), BF16),
            pltpu.VMEM((2, ffe, width), BF16),
            pltpu.VMEM((BLOCKS, 8, LANE), F32),
            pltpu.VMEM((BLOCKS, 8, LANE), F32),
            pltpu.VMEM((BLOCKS, LANE), F32),
            pltpu.VMEM((SEATS, BLOCKS, LANE), F32),
            pltpu.VMEM((LANE, TOK), jnp.int32),
            pltpu.VMEM((LANE, TOK), F32),
            dma((3,)),
            dma((8,)),
            dma((8,)),
            dma((21,)),
            dma((21,)),
            dma((chunks,)),
            dma((chunks,)),
            dma((BLOCKS,)),
            dma((BLOCKS,)),
            dma((BLOCKS,)),
            dma((BLOCKS,)),
            dma((8,)),
            dma((8,)),
            dma((2,)),
            dma((1,)),
        ],
        compiler_params=pltpu.CompilerParams(
            collective_id=0, has_side_effects=True, vmem_limit_bytes=63 * 1024 * 1024
        ),
        cost_estimate=pl.CostEstimate(
            flops=4 * slots * ffe * model, bytes_accessed=20_000_000, transcendentals=0
        ),
    )(routes.T, gate_values.T, kernel_row, grad_out, hidden[0], w_down[0])

    grad_hidden, grad_down = pl.pallas_call(
        finish,
        out_shape=(
            jax.ShapeDtypeStruct((slots, ffe), BF16),
            jax.ShapeDtypeStruct((ffe, model), BF16),
        ),
        in_specs=[hbm, hbm],
        out_specs=(hbm, hbm),
        scratch_shapes=[
            pltpu.VMEM((slots, ffe), BF16),
            pltpu.VMEM((ffe, model), BF16),
            dma((2, 12)),
        ],
        compiler_params=pltpu.CompilerParams(vmem_limit_bytes=63 * 1024 * 1024),
        cost_estimate=pl.CostEstimate(
            flops=0, bytes_accessed=17_000_000, transcendentals=0
        ),
    )(grad_hidden, grad_down)
    return grad_gates.T, grad_hidden[None], grad_down[None]


def solution(mesh):
    both = ("dp", "tensor")
    in_specs = (P(both, None), P(both, None), P(both, None), P(both, None, None), P(both, None, None))
    out_specs = (P(both, None), P(both, None, None), P(both, None, None))
    return jax.shard_map(local, mesh=mesh, in_specs=in_specs, out_specs=out_specs, check_vma=False)
```

time: 156 us -> 135 us (0.87)
  local copies, waits for them, and re-layouts: 12.4 us -> 0.6 us
  Pallas kernels: 140 us -> 133 us
    unnamed x4 -> x3, local copies, waits for them, and re-layouts: 12.4 us -> 0.6 us
    pallas_call x1 -> x2, Pallas kernels: 140 us -> 133 us  [the longest x1 127 us: local(): pl.pallas_call(body, out_shape=(jax.ShapeDtypeStruct((TOP, TOK), F32), ja...]
where the time goes in v2:
time: 135 us; the launch traced here: 134 us
  Pallas kernels  133 us (99%)
    pallas_call x1, Pallas kernels, local(): pl.pallas_call(body, out_shape=(jax.ShapeDtypeStruct((TOP, TOK), F32), ja...  127 us
    pallas_call x1, Pallas kernels, local(): pl.pallas_call(finish, out_shape=(jax.ShapeDtypeStruct((slots, ffe), BF16...  6.33 us

profile of v2, /device:TPU:1, one launch (start us, length us, event | category | flops | bytes accessed | tf_op | source)
XLA Modules:
  0.0 134.4 jit_solution(15938548536651023032)
XLA Ops:
  0.6 126.8 %shard_map.85 = (f32[8,128]{1,0:T(8,128)}, bf16[1536,768]{1,0:T(8,128)(2,1)}, bf16[768,4096]{1,0:T(8,128)(2,1)}) custom-call(s32[8,128]{1,0:T(8,128)} %bitcast.12, bf16[8,128]{1,0:T(8,128)(2,1)} %bitcast.13, s32[8,1536]{1,0:T(8,128)} %constant.2.clone.refs_2_, bf16[128,4096]{1,0:T(8,128)(2,1)} %refs_3_.1, bf16[1536,768]{1,0:T(8,128)(2,1)} %bitcast.10, ...), custom_call_target="tpu_custom_call" | custom-call | flops 19327352832 | bytes 20000000 | tf_op jit(solution)/shard_map/pallas_call | solution.py:565
  127.4 0.0 copy-start
  127.4 6.3 %shard_map.86 = (bf16[1536,768]{1,0:T(8,128)(2,1)}, bf16[768,4096]{1,0:T(8,128)(2,1)}) custom-call(bf16[1536,768]{1,0:T(8,128)(2,1)} %get-tuple-element.9.hidden_ref, bf16[768,4096]{1,0:T(8,128)(2,1)} %get-tuple-element.10.down_ref), custom_call_target="tpu_custom_call" | custom-call | bytes 17000000 | tf_op jit(solution)/shard_map/pallas_call | solution.py:622
  133.8 0.0 copy-done
  133.8 0.6 copy.10
Async XLA Ops:
  127.4 6.4 %copy-start = (f32[8,128]{1,0:T(8,128)S(1)}, f32[8,128]{1,0:T(8,128)}, u32[]{:S(2)}) copy-start(f32[8,128]{1,0:T(8,128)} %get-tuple-element.8) | copy-start | bytes 12292

commit v3 on v2

--- a/solution.py
+++ b/solution.py
@@ -140,6 +140,7 @@
     owner,
     count,
     in_sem,
+    far_sem,
     tab_send,
     tab_recv,
     rep_send,
@@ -166,7 +167,7 @@
     mine = seats[0] + 2 * seats[1] + 4 * seats[2]
     my_block = block_of(k, chip, 0)
     cores = (k, 1 - k)
-    order = [(n, rc) for n in (1, 2, 4, 3, 5, 6, 7, 0) for rc in (0, 1) if (n, rc) != (0, 0)]
+    order = [(n, rc) for rc in (0, 1) for n in (7, 3, 5, 6, 1, 2, 4, 0) if (n, rc) != (0, 0)]
 
     def receiver(n, rc):
         return reach(k, chip, n), cores[rc]
@@ -190,8 +191,8 @@
     load_weight.start()
 
     barrier = pltpu.get_barrier_semaphore()
-    greet = list(member_id.values()) + list(to_id.values())
-    greet += [from_id[n, 1] for n in range(1, 8)]
+    greet = [member_id[1 << d] for d in range(3)] + [to_id[1 << d, 0] for d in range(3)]
+    greet += [to_id[0, 1]]
     for who in greet:
         pl.semaphore_signal(barrier, inc=1, device_id=who, device_id_type=MESH)
 
@@ -204,26 +205,51 @@
     load_rows.wait()
     pl.semaphore_wait(barrier, len(greet))
 
-    def table_copy(f):
-        return pltpu.make_async_remote_copy(
-            src_ref=tables.at[mine],
-            dst_ref=tables.at[mine],
-            send_sem=tab_send.at[f],
-            recv_sem=tab_recv.at[f],
-            device_id=member_id[f],
-            device_id_type=MESH,
+    def tell(d):
+        pl.semaphore_signal(
+            far_sem.at[d], inc=1, device_id=to_id[1 << d, 0], device_id_type=MESH
         )
 
-    tiles = model // LANE
-    parts = [(0, 11), (11, 11), (22, tiles - 22)]
+    def hear(d):
+        pl.semaphore_wait(far_sem.at[d], 1)
+
+    def flipped(flips):
+        return sum((1 << d) * ((1 - seats[d]) if flips[d] else seats[d]) for d in range(3))
+
+    def table_copies(h):
+        copies = []
+        for c in range(1 << h):
+            ref = tables.at[flipped([d < h and (c >> d) & 1 for d in range(3)])]
+            at = (1 << h) - 1 + c
+            copies.append(
+                pltpu.make_async_remote_copy(
+                    src_ref=ref,
+                    dst_ref=ref,
+                    send_sem=tab_send.at[at],
+                    recv_sem=tab_recv.at[at],
+                    device_id=member_id[1 << h],
+                    device_id_type=MESH,
+                )
+            )
+        return copies
+
+    def send_tables(h):
+        for copy in table_copies(h):
+            copy.start()
+
+    def get_tables(h):
+        for copy in table_copies(h):
+            copy.wait_recv()
+
+    tiles = (6, 5, 5, 5, 6, model // LANE - 27)
+    starts = [sum(tiles[:p]) for p in range(7)]
+    groups = (range(0, 3), range(3, 6))
 
     def rep_copy(p, h, c):
-        slot = 0
-        for d in range(3):
-            hop = (d - p) % 3
-            slot = slot + (1 << d) * ((1 - seats[d]) if hop < h and (c >> hop) & 1 else seats[d])
+        hops = [(d - p) % 3 for d in range(3)]
+        slot = flipped([hop < h and (c >> hop) & 1 for hop in hops])
         at = p * 7 + (1 << h) - 1 + c
-        ref = tok.at[slot, :, pl.ds(parts[p][0] * LANE, parts[p][1] * LANE)]
+        ref = tok.at[slot, :, pl.ds(starts[p] * LANE, tiles[p] * LANE)]
         return pltpu.make_async_remote_copy(
             src_ref=ref,
             dst_ref=ref,
@@ -233,32 +259,61 @@
             device_id_type=MESH,
         )
 
-    def own(p):
+    def own(group):
         for h in range(3):
-            rep_copy(p, h, 0).start()
-
-    def forward_first(p):
-        rep_copy(p, 0, 0).wait_recv()
-        rep_copy(p, 1, 1).start()
-        rep_copy(p, 2, 1).start()
-        rep_copy(p, 1, 0).wait_recv()
-        rep_copy(p, 2, 2).start()
-
-    def forward_last(p):
-        rep_copy(p, 1, 1).wait_recv()
-        rep_copy(p, 2, 3).start()
-
-    def complete(p):
-        for c in range(4):
-            rep_copy(p, 2, c).wait_recv()
-
-    for f in range(1, 8):
-        table_copy(f).start()
-    for p in range(3):
-        own(p)
-
-    for f in range(1, 8):
-        table_copy(f).wait_recv()
+            for p in group:
+                rep_copy(p, h, 0).start()
+
+    def forward_first(group):
+        for p in group:
+            rep_copy(p, 0, 0).wait_recv()
+            rep_copy(p, 1, 1).start()
+        for p in group:
+            rep_copy(p, 2, 1).start()
+            rep_copy(p, 1, 0).wait_recv()
+            rep_copy(p, 2, 2).start()
+
+    def forward_last(group):
+        for p in group:
+            rep_copy(p, 1, 1).wait_recv()
+            rep_copy(p, 2, 3).start()
+
+    def complete(group):
+        for p in group:
+            for c in range(4):
+                rep_copy(p, 2, c).wait_recv()
+
+    span = 2 * LANE
+
+    def permute_hidden(start, stop):
+        @pl.loop(start, stop)
+        def _(i):
+            first = pl.multiple_of(i * span, span)
+            move = ones_where(kernel_row_ref[0:1, :] == iota((span, DEV * CAP), 0) + first)
+            moved = dot(move, hid[...])
+            hid_k[pl.ds(first, span), :] = moved.astype(BF16)
+            hid_t[:, pl.ds(first, span)] = moved.T.astype(BF16)
+
+    send_tables(0)
+    tell(0)
+    own(groups[0])
+    own(groups[1])
+    load_hidden.wait()
+    permute_hidden(0, 1)
+    get_tables(0)
+    send_tables(1)
+    hear(0)
+    tell(1)
+    permute_hidden(1, 2)
+    forward_first(groups[0])
+    get_tables(1)
+    send_tables(2)
+    hear(1)
+    tell(2)
+    permute_hidden(2, 4)
+    get_tables(2)
+    hear(2)
+
     gate_f[...] = tables[...].astype(F32)
     for n in range(8):
         for rc in range(2):
@@ -281,8 +336,8 @@
     for n, rc in order:
         gate_copy(n, rc).start()
 
-    for p in range(3):
-        forward_first(p)
+    forward_last(groups[0])
+    forward_first(groups[1])
 
     earlier = ones_where(iota((TOK, TOK), 0) < iota((TOK, TOK), 1))
     gates_all = gate_out[...].reshape(BLOCKS * SEATS, TOK)
@@ -298,23 +353,6 @@
             for m in range(4):
                 chosen = hit[rows] & (of[rows] == 4 * h + m)
                 select[h, d, :, m * TOK : (m + 1) * TOK] = ones_where(chosen)
-
-    load_hidden.wait()
-    span = 2 * LANE
-
-    def permute_hidden(start, stop):
-        @pl.loop(start, stop)
-        def _(i):
-            first = pl.multiple_of(i * span, span)
-            move = ones_where(kernel_row_ref[0:1, :] == iota((span, DEV * CAP), 0) + first)
-            moved = dot(move, hid[...])
-            hid_k[pl.ds(first, span), :] = moved.astype(BF16)
-            hid_t[:, pl.ds(first, span)] = moved.T.astype(BF16)
-
-    permute_hidden(0, 2)
-    for p in range(3):
-        forward_last(p)
-    permute_hidden(2, 6)
 
     def row_copy(q, n, rc):
         d = n * 2 + rc
@@ -340,9 +378,11 @@
             for n, rc in order:
                 row_copy(q, n, rc).start()
 
-    complete(0)
-    ready = [p[0] * LANE // width for p in parts] + [chunks]
-    exchange(ready[0], ready[1])
+    complete(groups[0])
+    exchange(0, 3)
+    forward_last(groups[1])
+    exchange(3, chunks // 2)
+    permute_hidden(4, 6)
 
     for n, rc in order:
         b = from_block[n, rc]
@@ -356,10 +396,8 @@
         column = jnp.sum(jnp.where(hit, gates, 0.0), axis=1, keepdims=True)
         gcol[b] = jnp.broadcast_to(column, (ROWS, LANE))
 
-    complete(1)
-    exchange(ready[1], ready[2])
-    complete(2)
-    exchange(ready[2], ready[3])
+    complete(groups[1])
+    exchange(chunks // 2, chunks)
 
     line = iota((LANE, TOK), 0)
     chips = []
@@ -391,17 +429,15 @@
 
     some = BLOCKS // 2
 
-    def project(q):
-        first = pl.multiple_of(q * width, width)
+    def arrive(q):
         all_rows = recv.at[q, pl.ds(0, BLOCKS - 1)]
         pltpu.make_async_copy(all_rows, all_rows, row_recv.at[q]).wait()
 
-        @pl.loop(0, 2)
-        def _(i):
-            got = recv[q, pl.ds(i * some, some)].reshape(some * ROWS, width)
-            back[pl.ds(i * some, some)] += dot(
-                got, weight[:, pl.ds(first, width)], ((1,), (1,))
-            ).reshape(some, ROWS, ffe)
+    def projected(q, i):
+        first = pl.multiple_of(q * width, width)
+        got = recv[q, pl.ds(i * some, some)].reshape(some * ROWS, width)
+        new = dot(got, weight[:, pl.ds(first, width)], ((1,), (1,)))
+        return back[pl.ds(i * some, some)] + new.reshape(some, ROWS, ffe)
 
     def weight_grad(q, slot):
         @pl.loop(0, BLOCKS)
@@ -415,7 +451,11 @@
     @pl.loop(0, chunks - 1)
     def _(q):
         slot = odd(q)
-        project(q)
+        arrive(q)
+
+        @pl.loop(0, 2)
+        def _(i):
+            back[pl.ds(i * some, some)] = projected(q, i)
 
         @pl.when(q >= 2)
         def _():
@@ -423,16 +463,19 @@
 
         weight_grad(q, slot)
 
-    project(chunks - 1)
-
-    @pl.loop(0, BLOCKS)
-    def _(b):
-        slots = hid_k[pl.ds(b * ROWS, ROWS), :].astype(F32) * back[b]
-        slots = jnp.sum(slots, axis=1, keepdims=True)
+    arrive(chunks - 1)
+
+    @pl.loop(0, 2)
+    def _(i):
+        total = projected(chunks - 1, i)
+        back[pl.ds(i * some, some)] = total
         row = iota((ROWS, LANE), 0)
-        lane = row + 4 * ((row * 171) >> 11)
-        line = jnp.sum(jnp.where(iota((ROWS, LANE), 1) == lane, slots, 0.0), axis=0, keepdims=True)
-        sg_out[b] = jnp.broadcast_to(line, (8, LANE))
+        hit = iota((ROWS, LANE), 1) == row + 4 * ((row * 171) >> 11)
+        for j in range(some):
+            rows = pl.ds(pl.multiple_of(i * some * ROWS, some * ROWS) + j * ROWS, ROWS)
+            slots = jnp.sum(hid_k[rows, :].astype(F32) * total[j], axis=1, keepdims=True)
+            line = jnp.sum(jnp.where(hit, slots, 0.0), axis=0, keepdims=True)
+            sg_out[i * some + j] = jnp.broadcast_to(line, (8, LANE))
 
     def slot_copy(n, rc):
         d = n * 2 + rc
@@ -495,10 +538,13 @@
     store_hidden = pltpu.make_async_copy(hid, grad_hidden_ref, hid_sem.at[0])
     store_hidden.start()
 
-    for p in range(3):
+    for p in range(6):
         for h in range(3):
             for c in range(1 << h):
                 rep_copy(p, h, c).wait_send()
+    for h in range(3):
+        for copy in table_copies(h):
+            copy.wait_send()
     for n, rc in order:
         gate_copy(n, rc).wait_send()
         slot_copy(n, rc).wait_send()
@@ -509,7 +555,6 @@
         pltpu.make_async_copy(all_rows, all_rows, row_send.at[q]).wait()
 
     for f in range(1, 8):
-        table_copy(f).wait_send()
         return_copy(f).wait_send()
 
     for f in range(1, 8):
@@ -527,12 +572,23 @@
     store_hidden.wait()
 
 
-def finish(hidden_ref, down_ref, grad_hidden_ref, grad_down_ref, hidden, down, sems):
-    pieces = 6
+def finish(
+    gates_ref,
+    hidden_ref,
+    down_ref,
+    grad_gates_ref,
+    grad_hidden_ref,
+    grad_down_ref,
+    gates,
+    hidden,
+    down,
+    sems,
+):
     loads, stores = [], []
-    for source, held, target in (
-        (down_ref, down, grad_down_ref),
-        (hidden_ref, hidden, grad_hidden_ref),
+    for source, held, target, pieces in (
+        (gates_ref, gates, grad_gates_ref, 1),
+        (down_ref, down, grad_down_ref, 6),
+        (hidden_ref, hidden, grad_hidden_ref, 4),
     ):
         rows = source.shape[0] // pieces
         for i in range(pieces):
@@ -596,10 +652,11 @@
             pltpu.VMEM((LANE, TOK), jnp.int32),
             pltpu.VMEM((LANE, TOK), F32),
             dma((3,)),
+            pltpu.SemaphoreType.REGULAR((3,)),
             dma((8,)),
             dma((8,)),
-            dma((21,)),
-            dma((21,)),
+            dma((42,)),
+            dma((42,)),
             dma((chunks,)),
             dma((chunks,)),
             dma((BLOCKS,)),
@@ -619,15 +676,17 @@
         ),
     )(routes.T, gate_values.T, kernel_row, grad_out, hidden[0], w_down[0])
 
-    grad_hidden, grad_down = pl.pallas_call(
+    grad_gates, grad_hidden, grad_down = pl.pallas_call(
         finish,
         out_shape=(
+            jax.ShapeDtypeStruct((TOP, TOK), F32),
             jax.ShapeDtypeStruct((slots, ffe), BF16),
             jax.ShapeDtypeStruct((ffe, model), BF16),
         ),
-        in_specs=[hbm, hbm],
-        out_specs=(hbm, hbm),
+        in_specs=[hbm, hbm, hbm],
+        out_specs=(hbm, hbm, hbm),
         scratch_shapes=[
+            pltpu.VMEM((TOP, TOK), F32),
             pltpu.VMEM((slots, ffe), BF16),
             pltpu.VMEM((ffe, model), BF16),
             dma((2, 12)),
@@ -636,7 +695,7 @@
         cost_estimate=pl.CostEstimate(
             flops=0, bytes_accessed=17_000_000, transcendentals=0
         ),
-    )(grad_hidden, grad_down)
+    )(grad_gates, grad_hidden, grad_down)
     return grad_gates.T, grad_hidden[None], grad_down[None]
 
 

time: 135 us -> 130 us (0.963)
  Pallas kernels: 133 us -> 129 us
    pallas_call x1, Pallas kernels: 127 us -> 123 us  [local(): pl.pallas_call(body, out_shape=(jax.ShapeDtypeStruct((TOP, TOK), F32), ja...]
where the time goes in v3:
time: 130 us
  Pallas kernels  129 us (99%)
    pallas_call x1, Pallas kernels, local(): pl.pallas_call(body, out_shape=(jax.ShapeDtypeStruct((TOP, TOK), F32), ja...  123 us
    pallas_call x1, Pallas kernels, local(): pl.pallas_call(finish, out_shape=(jax.ShapeDtypeStruct((TOP, TOK), F32),...  6.42 us

profile of v3, /device:TPU:1, one launch (start us, length us, event | category | flops | bytes accessed | tf_op | source)
XLA Modules:
  0.0 129.9 jit_solution(13847788025070971808)
XLA Ops:
  0.6 122.9 %shard_map.85 = (f32[8,128]{1,0:T(8,128)}, bf16[1536,768]{1,0:T(8,128)(2,1)}, bf16[768,4096]{1,0:T(8,128)(2,1)}) custom-call(s32[8,128]{1,0:T(8,128)} %bitcast.11, bf16[8,128]{1,0:T(8,128)(2,1)} %bitcast.13, s32[8,1536]{1,0:T(8,128)} %constant.2.clone.refs_2_, bf16[128,4096]{1,0:T(8,128)(2,1)} %refs_3_.1, bf16[1536,768]{1,0:T(8,128)(2,1)} %bitcast.9, ...), custom_call_target="tpu_custom_call" | custom-call | flops 19327352832 | bytes 20000000 | tf_op jit(solution)/shard_map/pallas_call | solution.py:621
  123.5 6.4 %shard_map.86 = (f32[8,128]{1,0:T(8,128)}, bf16[1536,768]{1,0:T(8,128)(2,1)}, bf16[768,4096]{1,0:T(8,128)(2,1)}) custom-call(f32[8,128]{1,0:T(8,128)} %get-tuple-element.9.gates_ref, bf16[1536,768]{1,0:T(8,128)(2,1)} %get-tuple-element.10.hidden_ref, bf16[768,4096]{1,0:T(8,128)(2,1)} %get-tuple-element.11.down_ref), custom_call_target="tpu_custom_call" | custom-call | bytes 17000000 | tf_op jit(solution)/shard_map/pallas_call | solution.py:679

commit v4 on v3

--- a/solution.py
+++ b/solution.py
@@ -107,20 +107,21 @@
 
 def kernel(
     chunks,
-    routes_ref,
-    gates_ref,
-    kernel_row_ref,
+    routes_in,
+    gates_in,
+    kernel_row_in,
     grad_ref,
     hidden_ref,
     weight_ref,
     grad_gates_ref,
-    grad_hidden_ref,
-    grad_down_ref,
+    hid,
+    weight,
+    routes_ref,
+    gates_ref,
+    kernel_row_ref,
     tok,
     stage,
     recv,
-    weight,
-    hid,
     hid_k,
     hid_t,
     back,
@@ -132,7 +133,6 @@
     gate_out,
     gate_in,
     scaled,
-    down,
     sg_out,
     sg_in,
     sg_pack,
@@ -153,8 +153,6 @@
     sg_recv,
     ret_send,
     ret_recv,
-    down_sem,
-    hid_sem,
 ):
     width = recv.shape[3]
     model = weight.shape[1]
@@ -185,16 +183,26 @@
 
     load_rows = pltpu.make_async_copy(grad_ref, tok.at[mine], in_sem.at[0])
     load_rows.start()
-    load_hidden = pltpu.make_async_copy(hidden_ref, hid, in_sem.at[1])
-    load_hidden.start()
-    load_weight = pltpu.make_async_copy(weight_ref, weight, in_sem.at[2])
-    load_weight.start()
+    load_small = [
+        pltpu.make_async_copy(routes_in, routes_ref, in_sem.at[3]),
+        pltpu.make_async_copy(gates_in, gates_ref, in_sem.at[4]),
+        pltpu.make_async_copy(kernel_row_in, kernel_row_ref, in_sem.at[5]),
+    ]
+    for load in load_small:
+        load.start()
 
     barrier = pltpu.get_barrier_semaphore()
     greet = [member_id[1 << d] for d in range(3)] + [to_id[1 << d, 0] for d in range(3)]
     greet += [to_id[0, 1]]
     for who in greet:
         pl.semaphore_signal(barrier, inc=1, device_id=who, device_id_type=MESH)
+
+    load_hidden = pltpu.make_async_copy(hidden_ref, hid, in_sem.at[1])
+    load_hidden.start()
+    load_weight = pltpu.make_async_copy(weight_ref, weight, in_sem.at[2])
+    load_weight.start()
+    for load in load_small:
+        load.wait()
 
     gates_t = gates_ref[...].astype(F32)
     table = jnp.zeros((DEV, TOK), F32)
@@ -421,12 +429,6 @@
     back[...] = jnp.zeros_like(back)
     load_weight.wait()
 
-    def down_copy(q, slot):
-        first = pl.multiple_of(q * width, width)
-        return pltpu.make_async_copy(
-            down.at[slot], grad_down_ref.at[:, pl.ds(first, width)], down_sem.at[slot]
-        )
-
     some = BLOCKS // 2
 
     def arrive(q):
@@ -439,29 +441,25 @@
         new = dot(got, weight[:, pl.ds(first, width)], ((1,), (1,)))
         return back[pl.ds(i * some, some)] + new.reshape(some, ROWS, ffe)
 
-    def weight_grad(q, slot):
+    def weight_grad(q):
+        first = pl.multiple_of(q * width, width)
+
         @pl.loop(0, BLOCKS)
         def _(b):
             wide = jnp.concatenate([gcol[b]] * (width // LANE), axis=1)
             scaled[pl.ds(b * ROWS, ROWS), :] = (recv[q, b].astype(F32) * wide).astype(BF16)
 
-        down[slot] = dot(hid_t[...], scaled[...]).astype(BF16)
-        down_copy(q, slot).start()
+        weight[:, pl.ds(first, width)] = dot(hid_t[...], scaled[...]).astype(BF16)
 
     @pl.loop(0, chunks - 1)
     def _(q):
-        slot = odd(q)
         arrive(q)
 
         @pl.loop(0, 2)
         def _(i):
             back[pl.ds(i * some, some)] = projected(q, i)
 
-        @pl.when(q >= 2)
-        def _():
-            down_copy(q - 2, slot).wait()
-
-        weight_grad(q, slot)
+        weight_grad(q)
 
     arrive(chunks - 1)
 
@@ -493,31 +491,7 @@
         slot_copy(n, rc).start()
     sg_in[0] = sg_out[my_block]
 
-    last = (chunks - 1) % 2
-    down_copy(chunks - 3, last).wait()
-    weight_grad(chunks - 1, last)
-
-    for n, rc in order:
-        slot_copy(n, rc).wait_recv()
-    for d in range(BLOCKS):
-        sg_pack[d : d + 1, :] = sg_in[d, 0:1, :]
-
-    def return_copy(f):
-        return pltpu.make_async_remote_copy(
-            src_ref=sg_pack,
-            dst_ref=sg_all.at[mine],
-            send_sem=ret_send.at[f],
-            recv_sem=ret_recv.at[f],
-            device_id=member_id[f],
-            device_id_type=MESH,
-        )
-
-    for f in range(1, 8):
-        return_copy(f).start()
-    sg_all[mine] = sg_pack[...]
-
-    for kk in range(2):
-
+    def order_hidden(kk):
         @pl.loop(0, 4)
         def _(i):
             for px in range(2):
@@ -534,9 +508,30 @@
                         m * CAP : (m + 1) * CAP
                     ]
 
+    weight_grad(chunks - 1)
+    order_hidden(0)
+
+    for n, rc in order:
+        slot_copy(n, rc).wait_recv()
+    for d in range(BLOCKS):
+        sg_pack[d : d + 1, :] = sg_in[d, 0:1, :]
+
+    def return_copy(f):
+        return pltpu.make_async_remote_copy(
+            src_ref=sg_pack,
+            dst_ref=sg_all.at[mine],
+            send_sem=ret_send.at[f],
+            recv_sem=ret_recv.at[f],
+            device_id=member_id[f],
+            device_id_type=MESH,
+        )
+
+    for f in range(1, 8):
+        return_copy(f).start()
+    sg_all[mine] = sg_pack[...]
+
+    order_hidden(1)
     hid[...] = natural[...].reshape(DEV * CAP, ffe).astype(BF16)
-    store_hidden = pltpu.make_async_copy(hid, grad_hidden_ref, hid_sem.at[0])
-    store_hidden.start()
 
     for p in range(6):
         for h in range(3):
@@ -567,39 +562,12 @@
         named = owner[...] == routes_ref[c : c + 1, :]
         grad_gates_ref[c : c + 1, :] = jnp.sum(jnp.where(named, value, 0.0), axis=0, keepdims=True)
 
-    down_copy(chunks - 2, 1 - last).wait()
-    down_copy(chunks - 1, last).wait()
-    store_hidden.wait()
-
-
-def finish(
-    gates_ref,
-    hidden_ref,
-    down_ref,
-    grad_gates_ref,
-    grad_hidden_ref,
-    grad_down_ref,
-    gates,
-    hidden,
-    down,
-    sems,
-):
-    loads, stores = [], []
-    for source, held, target, pieces in (
-        (gates_ref, gates, grad_gates_ref, 1),
-        (down_ref, down, grad_down_ref, 6),
-        (hidden_ref, hidden, grad_hidden_ref, 4),
-    ):
-        rows = source.shape[0] // pieces
-        for i in range(pieces):
-            at = pl.ds(i * rows, rows)
-            n = len(loads)
-            loads.append(pltpu.make_async_copy(source.at[at], held.at[at], sems.at[0, n]))
-            stores.append(pltpu.make_async_copy(held.at[at], target.at[at], sems.at[1, n]))
-            loads[-1].start()
-    for load, store in zip(loads, stores):
-        load.wait()
-        store.start()
+
+def finish(gates, hidden, down, grad_gates_ref, grad_hidden_ref, grad_down_ref, sems):
+    stores = []
+    for held, target in ((down, grad_down_ref), (hidden, grad_hidden_ref), (gates, grad_gates_ref)):
+        stores.append(pltpu.make_async_copy(held, target, sems.at[len(stores)]))
+        stores[-1].start()
     for store in stores:
         store.wait()
 
@@ -621,18 +589,19 @@
     grad_gates, grad_hidden, grad_down = pl.pallas_call(
         body,
         out_shape=(
-            jax.ShapeDtypeStruct((TOP, TOK), F32),
-            jax.ShapeDtypeStruct((slots, ffe), BF16),
-            jax.ShapeDtypeStruct((ffe, model), BF16),
+            pltpu.VMEM((TOP, TOK), F32),
+            pltpu.VMEM((slots, ffe), BF16),
+            pltpu.VMEM((ffe, model), BF16),
         ),
-        in_specs=[vmem] * 3 + [hbm] * 3,
-        out_specs=(vmem, hbm, hbm),
+        in_specs=[hbm] * 6,
+        out_specs=(vmem, vmem, vmem),
         scratch_shapes=[
+            pltpu.VMEM((TOP, TOK), jnp.int32),
+            pltpu.VMEM((TOP, TOK), BF16),
+            pltpu.VMEM((8, slots), jnp.int32),
             pltpu.VMEM((SEATS, TOK, model), BF16),
             pltpu.VMEM((chunks, BLOCKS, ROWS, width), BF16),
             pltpu.VMEM((chunks, BLOCKS, ROWS, width), BF16),
-            pltpu.VMEM((ffe, model), BF16),
-            pltpu.VMEM((slots, ffe), BF16),
             pltpu.VMEM((slots, ffe), BF16),
             pltpu.VMEM((ffe, slots), BF16),
             pltpu.VMEM((BLOCKS, ROWS, ffe), F32),
@@ -644,14 +613,13 @@
             pltpu.VMEM((BLOCKS, SEATS, TOK), F32),
             pltpu.VMEM((BLOCKS, SEATS, TOK), F32),
             pltpu.VMEM((slots, width), BF16),
-            pltpu.VMEM((2, ffe, width), BF16),
             pltpu.VMEM((BLOCKS, 8, LANE), F32),
             pltpu.VMEM((BLOCKS, 8, LANE), F32),
             pltpu.VMEM((BLOCKS, LANE), F32),
             pltpu.VMEM((SEATS, BLOCKS, LANE), F32),
             pltpu.VMEM((LANE, TOK), jnp.int32),
             pltpu.VMEM((LANE, TOK), F32),
-            dma((3,)),
+            dma((6,)),
             pltpu.SemaphoreType.REGULAR((3,)),
             dma((8,)),
             dma((8,)),
@@ -665,11 +633,9 @@
             dma((BLOCKS,)),
             dma((8,)),
             dma((8,)),
-            dma((2,)),
-            dma((1,)),
         ],
         compiler_params=pltpu.CompilerParams(
-            collective_id=0, has_side_effects=True, vmem_limit_bytes=63 * 1024 * 1024
+            collective_id=0, has_side_effects=True, vmem_limit_bytes=54 * 1024 * 1024
         ),
         cost_estimate=pl.CostEstimate(
             flops=4 * slots * ffe * model, bytes_accessed=20_000_000, transcendentals=0
@@ -683,15 +649,12 @@
             jax.ShapeDtypeStruct((slots, ffe), BF16),
             jax.ShapeDtypeStruct((ffe, model), BF16),
         ),
-        in_specs=[hbm, hbm, hbm],
+        in_specs=[vmem, vmem, vmem],
         out_specs=(hbm, hbm, hbm),
         scratch_shapes=[
-            pltpu.VMEM((TOP, TOK), F32),
-            pltpu.VMEM((slots, ffe), BF16),
-            pltpu.VMEM((ffe, model), BF16),
-            dma((2, 12)),
+            dma((3,)),
         ],
-        compiler_params=pltpu.CompilerParams(vmem_limit_bytes=63 * 1024 * 1024),
+        compiler_params=pltpu.CompilerParams(vmem_limit_bytes=2 * 1024 * 1024),
         cost_estimate=pl.CostEstimate(
             flops=0, bytes_accessed=17_000_000, transcendentals=0
         ),

time: 130 us -> 126 us (0.969)
  Pallas kernels: 129 us -> 125 us
    pallas_call x1, Pallas kernels: 6.42 us -> 3.5 us  [local(): pl.pallas_call(finish, out_shape=(jax.ShapeDtypeStruct((TOP, TOK), F32),...]
where the time goes in v4:
time: 126 us
  Pallas kernels  125 us (99%)
    pallas_call x1, Pallas kernels, local(): pl.pallas_call(body, out_shape=(pltpu.VMEM((TOP, TOK), F32), pltpu.VMEM((...  122 us
    pallas_call x1, Pallas kernels, local(): pl.pallas_call(finish, out_shape=(jax.ShapeDtypeStruct((TOP, TOK), F32),...  3.5 us

profile of v4, /device:TPU:1, one launch (start us, length us, event | category | flops | bytes accessed | tf_op | source)
XLA Modules:
  0.0 125.8 jit_solution(15972539991724993597)
XLA Ops:
  0.6 121.7 %shard_map.85 = (f32[8,128]{1,0:T(8,128)S(1)}, bf16[1536,768]{1,0:T(8,128)(2,1)S(1)}, bf16[768,4096]{1,0:T(8,128)(2,1)S(1)}) custom-call(s32[8,128]{1,0:T(8,128)} %bitcast.11, bf16[8,128]{1,0:T(8,128)(2,1)} %bitcast.13, s32[8,1536]{1,0:T(8,128)} %constant.2.clone.refs_2_, bf16[128,4096]{1,0:T(8,128)(2,1)} %refs_3_.1, bf16[1536,768]{1,0:T(8,128)(2,1)} %bitcast.9, ...), custom_call_target="tpu_custom_call" | custom-call | flops 19327352832 | bytes 20000000 | tf_op jit(solution)/shard_map/pallas_call | solution.py:589
  122.3 3.5 %shard_map.86 = (f32[8,128]{1,0:T(8,128)}, bf16[1536,768]{1,0:T(8,128)(2,1)}, bf16[768,4096]{1,0:T(8,128)(2,1)}) custom-call(f32[8,128]{1,0:T(8,128)S(1)} %get-tuple-element.9.gates, bf16[1536,768]{1,0:T(8,128)(2,1)S(1)} %get-tuple-element.10.hidden, bf16[768,4096]{1,0:T(8,128)(2,1)S(1)} %get-tuple-element.11.down), custom_call_target="tpu_custom_call" | custom-call | bytes 17000000 | tf_op jit(solution)/shard_map/pallas_call | solution.py:645

commit v5 on v4

--- a/solution.py
+++ b/solution.py
@@ -249,7 +249,7 @@
         for copy in table_copies(h):
             copy.wait_recv()
 
-    tiles = (6, 5, 5, 5, 6, model // LANE - 27)
+    tiles = (7, 7, 6, 4, 4, model // LANE - 28)
     starts = [sum(tiles[:p]) for p in range(7)]
     groups = (range(0, 3), range(3, 6))
 
@@ -278,6 +278,7 @@
             rep_copy(p, 1, 1).start()
         for p in group:
             rep_copy(p, 2, 1).start()
+        for p in group:
             rep_copy(p, 1, 0).wait_recv()
             rep_copy(p, 2, 2).start()
 
@@ -387,9 +388,9 @@
                 row_copy(q, n, rc).start()
 
     complete(groups[0])
-    exchange(0, 3)
     forward_last(groups[1])
-    exchange(3, chunks // 2)
+    first = starts[3] * LANE // width
+    exchange(0, first)
     permute_hidden(4, 6)
 
     for n, rc in order:
@@ -405,7 +406,7 @@
         gcol[b] = jnp.broadcast_to(column, (ROWS, LANE))
 
     complete(groups[1])
-    exchange(chunks // 2, chunks)
+    exchange(first, chunks)
 
     line = iota((LANE, TOK), 0)
     chips = []
@@ -565,9 +566,17 @@
 
 def finish(gates, hidden, down, grad_gates_ref, grad_hidden_ref, grad_down_ref, sems):
     stores = []
-    for held, target in ((down, grad_down_ref), (hidden, grad_hidden_ref), (gates, grad_gates_ref)):
-        stores.append(pltpu.make_async_copy(held, target, sems.at[len(stores)]))
-        stores[-1].start()
+    for held, target, pieces in (
+        (down, grad_down_ref, 8),
+        (hidden, grad_hidden_ref, 4),
+        (gates, grad_gates_ref, 1),
+    ):
+        rows = held.shape[0] // pieces
+        for i in range(pieces):
+            at = pl.ds(i * rows, rows)
+            sem = sems.at[len(stores)]
+            stores.append(pltpu.make_async_copy(held.at[at], target.at[at], sem))
+            stores[-1].start()
     for store in stores:
         store.wait()
 
@@ -652,7 +661,7 @@
         in_specs=[vmem, vmem, vmem],
         out_specs=(hbm, hbm, hbm),
         scratch_shapes=[
-            dma((3,)),
+            dma((13,)),
         ],
         compiler_params=pltpu.CompilerParams(vmem_limit_bytes=2 * 1024 * 1024),
         cost_estimate=pl.CostEstimate(

time: 126 us -> 126 us (level)
  no operation moved by 1% of the time
where the time goes in v5:
time: 126 us
  Pallas kernels  125 us (99%)
    pallas_call x1, Pallas kernels, local(): pl.pallas_call(body, out_shape=(pltpu.VMEM((TOP, TOK), F32), pltpu.VMEM((...  121 us
    pallas_call x1, Pallas kernels, local(): pl.pallas_call(finish, out_shape=(jax.ShapeDtypeStruct((TOP, TOK), F32),...  3.49 us

profile of v5, /device:TPU:1, one launch (start us, length us, event | category | flops | bytes accessed | tf_op | source)
XLA Modules:
  0.0 125.5 jit_solution(9086314616553399145)
XLA Ops:
  0.6 121.4 %shard_map.85 = (f32[8,128]{1,0:T(8,128)S(1)}, bf16[1536,768]{1,0:T(8,128)(2,1)S(1)}, bf16[768,4096]{1,0:T(8,128)(2,1)S(1)}) custom-call(s32[8,128]{1,0:T(8,128)} %bitcast.11, bf16[8,128]{1,0:T(8,128)(2,1)} %bitcast.13, s32[8,1536]{1,0:T(8,128)} %constant.2.clone.refs_2_, bf16[128,4096]{1,0:T(8,128)(2,1)} %refs_3_.1, bf16[1536,768]{1,0:T(8,128)(2,1)} %bitcast.9, ...), custom_call_target="tpu_custom_call" | custom-call | flops 19327352832 | bytes 20000000 | tf_op jit(solution)/shard_map/pallas_call | solution.py:598
  122.1 3.5 %shard_map.86 = (f32[8,128]{1,0:T(8,128)}, bf16[1536,768]{1,0:T(8,128)(2,1)}, bf16[768,4096]{1,0:T(8,128)(2,1)}) custom-call(f32[8,128]{1,0:T(8,128)S(1)} %get-tuple-element.9.gates, bf16[1536,768]{1,0:T(8,128)(2,1)S(1)} %get-tuple-element.10.hidden, bf16[768,4096]{1,0:T(8,128)(2,1)S(1)} %get-tuple-element.11.down), custom_call_target="tpu_custom_call" | custom-call | bytes 17000000 | tf_op jit(solution)/shard_map/pallas_call | solution.py:654
